TPU v7x, 512 devices: a whole 4x8x8 slice. The times are simulated.
512 devices in a mesh: dp: 64 (over z, y), tensor: 8 (over x, core).
Axes of the slice: x: 4, y: 8, z: 8, core: 2. Of those that a mesh axis runs over, the one named last changes fastest.
Arguments:
- queries: bfloat16 [8192, 4, 8192], P('dp', None, 'tensor'), may hold values from -15 to 15
- grad_out: bfloat16 [8192, 4, 8192], P('dp', None, 'tensor'), may hold values from -6 to 6
- image_keys: bfloat16 [64, 768, 1024], P('dp', None, 'tensor'), may hold values from -4 to 4
- image_values: bfloat16 [64, 768, 1024], P('dp', None, 'tensor'), may hold values from -6 to 6
- gate_logits: float32 [64], P('tensor'), may hold values from -1.5 to 1.5
- tile_counts: int32 [64], P('dp'), may hold values from 1 to 3
- owners: int32 [8192, 1], P('dp'), may hold values from 0 to 63; in each aligned block of 128 rows (0 to 127, 128 to 255, ...) at most 3 rows name the same one
- text_only: int32 [8192], P('dp'), may hold values 0 or 1
Outputs:
- grad_queries: bfloat16 [8192, 4, 8192], P('dp', None, 'tensor')
- grad_keys: bfloat16 [64, 768, 1024], P('dp', None, 'tensor')
- grad_values: bfloat16 [64, 768, 1024], P('dp', None, 'tensor')
Inputs may be any that keep to these rules, and one draw needn't show every extreme that they name: `owners`: of the rows of one device at most 3 name the same image, a bound that some block reaches of them.
All inputs are finite; a program needn't handle non-finite values. No bound on the sum of `text_only` on one device may be relied on, other than what follows from the above.
Results may differ from a plain program's by a relative error of at most 0.02.
Values may be sent and summed in bfloat16 or wider, within the bound.
No kernel may reach another device: no remote copies, remote signals or barrier semaphores. Data moves between devices by JAX's collectives and lax.ppermute only.
A program may use at most 64 MiB of HBM per device.

v0:
```python
import jax
import jax.numpy as jnp
from jax import lax
from jax.sharding import PartitionSpec as P

HEAD = 128
TILE = 256


def attend(query_block, grad_block, key_rows, value_rows, key_live, gate_scale):
    slot_count = query_block.shape[0]
    token_count = query_block.shape[1]
    kv_local = key_rows.shape[1] // HEAD
    group_size = query_block.shape[2] // (kv_local * HEAD)
    flat_tokens = slot_count * token_count
    score_scale = HEAD ** (-0.5)
    query_four = query_block.reshape(flat_tokens, kv_local, group_size, HEAD)
    grad_four = grad_block.reshape(flat_tokens, kv_local, group_size, HEAD)
    key_three = key_rows.reshape(-1, kv_local, HEAD)
    value_three = value_rows.reshape(-1, kv_local, HEAD)
    scores = (
        jnp.einsum("ncgd,kcd->cgnk", query_four, key_three, preferred_element_type=jnp.float32)
        * score_scale
    )
    scores = jnp.where(key_live, scores, -1e30)
    largest = jnp.max(scores, axis=-1, keepdims=True)
    expo_terms = jnp.exp(scores - largest)
    probs = expo_terms / jnp.sum(expo_terms, axis=-1, keepdims=True)
    head_gate = gate_scale.reshape(kv_local, group_size)[:, :, None, None]
    weighted = (head_gate * probs).astype(jnp.bfloat16)
    grad_probs = jnp.einsum(
        "ncgd,kcd->cgnk", grad_four, value_three, preferred_element_type=jnp.float32
    )
    row_delta = jnp.sum(probs * grad_probs, axis=-1, keepdims=True)
    grad_scores = (probs * (grad_probs - row_delta) * head_gate * score_scale).astype(jnp.bfloat16)
    grad_query = jnp.einsum(
        "cgnk,kcd->ncgd", grad_scores, key_three, preferred_element_type=jnp.float32
    )
    grad_query = grad_query.astype(jnp.bfloat16).reshape(slot_count, -1)
    grad_key = jnp.einsum(
        "cgnk,ncgd->kcd", grad_scores, query_four, preferred_element_type=jnp.float32
    )
    grad_value = jnp.einsum(
        "cgnk,ncgd->kcd", weighted, grad_four, preferred_element_type=jnp.float32
    )
    return (grad_query, grad_key.reshape(key_rows.shape), grad_value.reshape(value_rows.shape))


def on_device(
    queries, grad_out, image_keys, image_values, gate_logits, tile_counts, owners, text_only
):
    row_count, token_count, feature_width = queries.shape
    peer_count = lax.axis_size("dp")
    capacity = max(2, (3 * row_count + 2 * peer_count - 1) // (2 * peer_count))
    slot_total = peer_count * capacity
    slot_block = 16
    live_rows = (1 - text_only).astype(jnp.float32)
    target = owners[:, 0]
    member = (target[:, None] == jnp.arange(peer_count, dtype=jnp.int32)[None, :]).astype(
        jnp.float32
    )
    member = member * live_rows[:, None]
    earlier = jnp.cumsum(member, axis=0) - member
    rank_rows = jnp.sum(earlier * member, axis=1).astype(jnp.int32)
    slot_of = target * capacity + rank_rows
    placing = jnp.logical_and(
        slot_of[None, :] == jnp.arange(slot_total, dtype=jnp.int32)[:, None],
        live_rows[None, :] > 0.5,
    ).astype(jnp.bfloat16)
    send_query = jnp.dot(
        placing, queries.reshape(row_count, -1), preferred_element_type=jnp.float32
    ).astype(jnp.bfloat16)
    send_grad = jnp.dot(
        placing, grad_out.reshape(row_count, -1), preferred_element_type=jnp.float32
    ).astype(jnp.bfloat16)
    send_valid = jnp.sum(placing.astype(jnp.float32), axis=1).astype(jnp.bfloat16)
    recv_query, recv_grad, recv_valid = (
        lax.all_to_all(send_query, "dp", split_axis=0, concat_axis=0, tiled=True),
        lax.all_to_all(send_grad, "dp", split_axis=0, concat_axis=0, tiled=True),
        lax.all_to_all(send_valid, "dp", split_axis=0, concat_axis=0, tiled=True),
    )
    key_rows = image_keys[0]
    value_rows = image_values[0]
    key_live = jnp.arange(key_rows.shape[0], dtype=jnp.int32) < tile_counts[0] * TILE
    gate_scale = jnp.tanh(gate_logits)

    def one_block(block_id, running):
        grad_key, grad_value, grad_slots = running
        block_start = block_id * slot_block
        query_block = lax.dynamic_slice_in_dim(recv_query, block_start, slot_block, 0)
        grad_block = lax.dynamic_slice_in_dim(recv_grad, block_start, slot_block, 0)
        query_block = query_block.reshape(slot_block, token_count, feature_width)
        grad_block = grad_block.reshape(slot_block, token_count, feature_width)
        block_query, block_key, block_value = attend(
            query_block, grad_block, key_rows, value_rows, key_live, gate_scale
        )
        grad_slots = lax.dynamic_update_slice_in_dim(grad_slots, block_query, block_start, 0)
        return (grad_key + block_key, grad_value + block_value, grad_slots)

    initial = (
        jnp.zeros(key_rows.shape, jnp.float32),
        jnp.zeros(value_rows.shape, jnp.float32),
        jnp.zeros(recv_query.shape, jnp.bfloat16),
    )
    grad_key, grad_value, grad_slots = lax.fori_loop(
        0, slot_total // slot_block, one_block, initial
    )
    returned = lax.all_to_all(grad_slots, "dp", split_axis=0, concat_axis=0, tiled=True)
    grad_rows = jnp.dot(placing.T, returned, preferred_element_type=jnp.float32).astype(
        jnp.bfloat16
    )
    grad_rows = grad_rows.reshape(row_count, token_count, feature_width)
    return (grad_rows, grad_key.astype(jnp.bfloat16)[None], grad_value.astype(jnp.bfloat16)[None])


def solution(mesh):
    placed = (
        P("dp", None, "tensor"),
        P("dp", None, "tensor"),
        P("dp", None, "tensor"),
        P("dp", None, "tensor"),
        P("tensor"),
        P("dp"),
        P("dp", None),
        P("dp"),
    )
    return jax.shard_map(
        on_device,
        mesh=mesh,
        in_specs=placed,
        out_specs=(P("dp", None, "tensor"), P("dp", None, "tensor"), P("dp", None, "tensor")),
        check_vma=False,
    )
```

profile of v0, /device:TPU:6, one launch (start us, length us, event | category | flops | bytes accessed | tf_op | source)
XLA Modules:
  0.0 267.4 jit_solution(16863502211492614272)
XLA Ops:
  2.9 0.8 fusion.27
  4.4 1.6 copy.32
  6.6 2.4 all_to_all.24
  8.9 16.6 %all-to-all-start = ((bf16[64,3,4096]{2,1,0:T(4,128)(2,1)}), bf16[64,3,4096]{2,1,0:T(4,128)(2,1)S(1)}, u32[]{:S(2)}, u32[]{:S(2)}) async-start(bf16[64,3,4096]{2,1,0:T(4,128)(2,1)} %all_to_all.24), calls=%async_computation | async-start | bytes 4194304 | tf_op jit(solution)/shard_map/all_to_all | solution.py:78
  25.5 1.6 copy.33
  27.1 1.7 convolution_convert_fusion
  28.8 4.1 %all_to_all.27 = bf16[64,3,4096]{2,1,0:T(4,128)(2,1)} reshape(bf16[192,4096]{1,0:T(8,128)(2,1)} %convolution_convert_fusion) | data formatting | bytes 3145728 | tf_op jit(solution)/shard_map/all_to_all | solution.py:79
  32.9 44.9 %all-to-all-done = bf16[64,3,4096]{2,1,0:T(4,128)(2,1)S(1)} async-done(((bf16[64,3,4096]{2,1,0:T(4,128)(2,1)}), bf16[64,3,4096]{2,1,0:T(4,128)(2,1)S(1)}, u32[]{:S(2)}, u32[]{:S(2)}) %all-to-all-start) | async-done | bytes 1572896 | tf_op jit(solution)/shard_map/all_to_all | solution.py:78
  77.9 9.4 %all-to-all-start.1 = ((bf16[64,3,4096]{2,1,0:T(4,128)(2,1)}), bf16[64,3,4096]{2,1,0:T(4,128)(2,1)}, u32[]{:S(2)}, u32[]{:S(2)}) async-start(bf16[64,3,4096]{2,1,0:T(4,128)(2,1)} %all_to_all.27), calls=%async_computation.1 | async-start | bytes 4194304 | tf_op jit(solution)/shard_map/all_to_all | solution.py:79
  87.9 2.5 all_to_all.26
  90.5 48.2 %all-to-all-done.1 = bf16[64,3,4096]{2,1,0:T(4,128)(2,1)} async-done(((bf16[64,3,4096]{2,1,0:T(4,128)(2,1)}), bf16[64,3,4096]{2,1,0:T(4,128)(2,1)}, u32[]{:S(2)}, u32[]{:S(2)}) %all-to-all-start.1) | async-done | bytes 1572896 | tf_op jit(solution)/shard_map/all_to_all | solution.py:79
  138.7 4.3 %all_to_all.29 = bf16[192,4096]{1,0:T(8,128)(2,1)} reshape(bf16[64,3,4096]{2,1,0:T(4,128)(2,1)} %all-to-all-done.1) | data formatting | bytes 3145728 | tf_op jit(solution)/shard_map/all_to_all | solution.py:79
  144.0 58.0 %while.18 = (s32[]{:T(128)}, f32[768,128]{0,1:T(8,128)S(1)}, f32[768,128]{0,1:T(8,128)S(1)}, bf16[192,4096]{1,0:T(8,128)(2,1)S(1)}, bf16[192,4096]{1,0:T(8,128)(...) while((s32[]{:T(128)}, f32[768,128]{0,1:T(8,128)S(1)}, ...), condition=%wide.region_6.7_spmd.clone, body=%wide.region_2.6_spmd.clone.sunk | while | flops 511573248 | bytes 18308880 | solution.py:105
  144.0 1.0 constant_dynamic-slice_fusion.3
  148.8 1.0 constant_dynamic-slice_fusion.3
  153.7 1.0 constant_dynamic-slice_fusion.3
  158.5 1.0 constant_dynamic-slice_fusion.3
  163.3 1.0 constant_dynamic-slice_fusion.3
  168.2 1.0 constant_dynamic-slice_fusion.3
  173.0 1.0 constant_dynamic-slice_fusion.3
  177.8 1.0 constant_dynamic-slice_fusion.3
  182.7 1.0 constant_dynamic-slice_fusion.3
  187.5 1.0 constant_dynamic-slice_fusion.3
  192.3 1.0 constant_dynamic-slice_fusion.3
  197.2 1.0 constant_dynamic-slice_fusion.3
  202.0 2.4 all_to_all.30
  204.3 6.5 %all-to-all-start.2 = ((bf16[64,3,4096]{2,1,0:T(4,128)(2,1)}), bf16[64,3,4096]{2,1,0:T(4,128)(2,1)S(1)}, u32[]{:S(2)}, u32[]{:S(2)}) async-start(bf16[64,3,4096]{2,1,0:T(4,128)(2,1)} %all_to_all.30), calls=%async_computation.2 | async-start | bytes 4194304 | tf_op jit(solution)/shard_map/all_to_all | solution.py:108
  210.8 0.8 copy.24
  212.5 48.9 %all-to-all-done.2 = bf16[64,3,4096]{2,1,0:T(4,128)(2,1)S(1)} async-done(((bf16[64,3,4096]{2,1,0:T(4,128)(2,1)}), bf16[64,3,4096]{2,1,0:T(4,128)(2,1)S(1)}, u32[]{:S(2)}, u32[]{:S(2)}) %all-to-all-start.2) | async-done | bytes 1572896 | tf_op jit(solution)/shard_map/all_to_all | solution.py:108
  261.4 2.5 all_to_all.32
  263.9 1.9 convolution_convert_fusion.2
  265.8 1.6 reshape.152
  (185 shorter events, 50.0 us)
Async XLA Ops:
  8.9 69.0 %all-to-all-start = ((bf16[64,3,4096]{2,1,0:T(4,128)(2,1)}), bf16[64,3,4096]{2,1,0:T(4,128)(2,1)S(1)}, u32[]{:S(2)}, u32[]{:S(2)}) async-start(bf16[64,3,4096]{2,1,0:T(4,128)(2,1)} %all_to_all.24), calls=%async_computation | async-start | bytes 4194304 | tf_op jit(solution)/shard_map/all_to_all | solution.py:78
  32.9 55.0 %copy-start.2 = (f32[8]{0:T(128)S(1)}, f32[8]{0:T(128)}, u32[]{:S(2)}) copy-start(f32[8]{0:T(128)} %param.14) | copy-start | bytes 100
  77.9 60.8 %all-to-all-start.1 = ((bf16[64,3,4096]{2,1,0:T(4,128)(2,1)}), bf16[64,3,4096]{2,1,0:T(4,128)(2,1)}, u32[]{:S(2)}, u32[]{:S(2)}) async-start(bf16[64,3,4096]{2,1,0:T(4,128)(2,1)} %all_to_all.27), calls=%async_computation.1 | async-start | bytes 4194304 | tf_op jit(solution)/shard_map/all_to_all | solution.py:79
  143.0 0.9 copy-start
  143.0 1.0 copy-start.1
  204.3 57.0 %all-to-all-start.2 = ((bf16[64,3,4096]{2,1,0:T(4,128)(2,1)}), bf16[64,3,4096]{2,1,0:T(4,128)(2,1)S(1)}, u32[]{:S(2)}, u32[]{:S(2)}) async-start(bf16[64,3,4096]{2,1,0:T(4,128)(2,1)} %all_to_all.30), calls=%async_computation.2 | async-start | bytes 4194304 | tf_op jit(solution)/shard_map/all_to_all | solution.py:108
where the time goes:
time: 268 us; the launch traced here: 267 us
  waiting for transfers between devices  142 us (53%)
  local copies, waits for them, and re-layouts  41.3 us (15%)
  matrix products  33.6 us (13%)
  starting transfers between devices  32.5 us (12%)
  other arithmetic  15.3 us (6%)
    all_to_all x1, waiting for transfers between devices, on_device(): lax.all_to_all(grad_slots, 'dp', split_axis=0, concat_axis=0, tiled=True)  48.9 us
    all_to_all x1, waiting for transfers between devices, on_device(): lax.all_to_all(send_grad, 'dp', split_axis=0, concat_axis=0, tiled=True)  48.2 us
    all_to_all x1, waiting for transfers between devices, on_device(): lax.all_to_all(send_query, 'dp', split_axis=0, concat_axis=0, tiled=True)  44.9 us
    all_to_all x1, starting transfers between devices, on_device(): lax.all_to_all(send_query, 'dp', split_axis=0, concat_axis=0, tiled=True)  16.6 us
    dynamic_slice x12, local copies, waits for them, and re-layouts, one_block(): grad_block = lax.dynamic_slice_in_dim(recv_grad, block_start, slot_block, 0)  11.9 us
    all_to_all x1, starting transfers between devices, on_device(): lax.all_to_all(send_grad, 'dp', split_axis=0, concat_axis=0, tiled=True)  9.36 us
    all_to_all x2, local copies, waits for them, and re-layouts, on_device(): lax.all_to_all(send_grad, 'dp', split_axis=0, concat_axis=0, tiled=True)  8.38 us
    dot_general x12, matrix products, attend(): jnp.einsum('ncgd,kcd->cgnk', grad_four, value_three, preferred_element_ty...  7.91 us
  transfers between devices with their start and end apart: 3, of which 3 were waited for; matrix products, arithmetic and copies ran while one was open for 2% of the time, Pallas kernels for 0%

commit v1 on v0

v1 whole, which is shorter than its diff:
```python
import math

import jax
import jax.numpy as jnp
from jax import lax
from jax.experimental import pallas as pl
from jax.experimental.pallas import tpu as pltpu
from jax.sharding import PartitionSpec as P

HEAD = 128
TILE = 256
CAP = 3
SUB = 256
GROUP = 16
SCALE = HEAD ** (-0.5)


def pack_kernel(
    owner_hbm, text_hbm, query_hbm, grad_hbm, send_hbm, slot_ref,
    owners, texts, count, place_of, query_rows, grad_rows, query_slots, grad_slots,
    in_sems, out_sems,
):
    rows = query_rows.shape[0]
    peers = query_slots.shape[0] - 1
    owner_copy = pltpu.make_async_copy(owner_hbm, owners, in_sems.at[0])
    text_copy = pltpu.make_async_copy(text_hbm, texts, in_sems.at[1])
    query_copy = pltpu.make_async_copy(query_hbm, query_rows, in_sems.at[2])
    grad_copy = pltpu.make_async_copy(grad_hbm, grad_rows, in_sems.at[3])
    owner_copy.start()
    text_copy.start()
    query_copy.start()
    grad_copy.start()
    for peer in range(peers):
        count[peer] = 0
    query_slots[...] = jnp.zeros(query_slots.shape, query_slots.dtype)
    grad_slots[...] = jnp.zeros(grad_slots.shape, grad_slots.dtype)
    owner_copy.wait()
    text_copy.wait()

    @pl.loop(0, rows // 8)
    def _(group):
        for inner in range(8):
            row = group * 8 + inner
            owner = owners[row]
            live = texts[row] == 0
            rank = count[owner]
            count[owner] = rank + jnp.where(live, 1, 0)
            place_of[row] = jnp.where(live, owner * 4 + rank, peers * 4)
            slot_ref[row] = jnp.where(live, owner * CAP + rank, -1)

    out_copies = []
    for which, (copy, source, target) in enumerate(
        ((query_copy, query_rows, query_slots), (grad_copy, grad_rows, grad_slots))
    ):
        copy.wait()

        @pl.loop(0, rows // 8)
        def _(group, source=source, target=target):
            for inner in range(8):
                row = group * 8 + inner
                place = place_of[row]
                target[place >> 2, place & 3] = source[row]

        out = pltpu.make_async_copy(
            target.at[pl.ds(0, peers)],
            send_hbm.at[:, pl.ds(which * CAP, CAP)],
            out_sems.at[which],
        )
        out.start()
        out_copies.append(out)
    for out in out_copies:
        out.wait()


def pack(owners, text_only, queries, grad_out, peers):
    rows = queries.shape[0]
    slab = queries.shape[1:]
    hbm = pl.BlockSpec(memory_space=pltpu.HBM)
    padded = (peers + 1, CAP) + slab
    return pl.pallas_call(
        pack_kernel,
        out_shape=(
            jax.ShapeDtypeStruct((peers, 2 * CAP) + slab, jnp.bfloat16),
            jax.ShapeDtypeStruct((rows,), jnp.int32),
        ),
        in_specs=[hbm, hbm, hbm, hbm],
        out_specs=(hbm, pl.BlockSpec(memory_space=pltpu.SMEM)),
        scratch_shapes=[
            pltpu.SMEM((rows,), jnp.int32),
            pltpu.SMEM((rows,), jnp.int32),
            pltpu.SMEM((peers,), jnp.int32),
            pltpu.SMEM((rows,), jnp.int32),
            pltpu.VMEM((rows,) + slab, jnp.bfloat16),
            pltpu.VMEM((rows,) + slab, jnp.bfloat16),
            pltpu.VMEM(padded, jnp.bfloat16),
            pltpu.VMEM(padded, jnp.bfloat16),
            pltpu.SemaphoreType.DMA((4,)),
            pltpu.SemaphoreType.DMA((2,)),
        ],
        compiler_params=pltpu.CompilerParams(vmem_limit_bytes=60 * 2**20),
        name="pack_rows",
    )(owners, text_only, queries, grad_out)


def unpack_kernel(slot_ref, slots_ref, out_hbm, rows_ref, sems):
    rows = rows_ref.shape[0]
    parts = sems.shape[0]
    share = rows // parts
    copies = []
    for part in range(parts):
        @pl.loop(0, share // 8)
        def _(group, part=part):
            for inner in range(8):
                row = part * share + group * 8 + inner
                slot = slot_ref[row]
                slab = slots_ref[jnp.maximum(slot, 0)]
                rows_ref[row] = jnp.where(slot >= 0, slab, jnp.zeros_like(slab))

        piece = pl.ds(part * share, share)
        copy = pltpu.make_async_copy(rows_ref.at[piece], out_hbm.at[piece], sems.at[part])
        copy.start()
        copies.append(copy)
    for copy in copies:
        copy.wait()


def unpack(slot_of, slots):
    rows = (slot_of.shape[0],) + slots.shape[1:]
    return pl.pallas_call(
        unpack_kernel,
        out_shape=jax.ShapeDtypeStruct(rows, jnp.bfloat16),
        in_specs=[pl.BlockSpec(memory_space=pltpu.SMEM), pl.BlockSpec(memory_space=pltpu.VMEM)],
        out_specs=pl.BlockSpec(memory_space=pltpu.HBM),
        scratch_shapes=[pltpu.VMEM(rows, jnp.bfloat16), pltpu.SemaphoreType.DMA((4,))],
        compiler_params=pltpu.CompilerParams(vmem_limit_bytes=48 * 2**20),
        name="unpack_rows",
    )(slot_of, slots)


def nt_dot(a, b):
    return lax.dot_general(a, b, (((1,), (1,)), ((), ())), preferred_element_type=jnp.float32)


def nn_dot(a, b):
    return jnp.dot(a, b, preferred_element_type=jnp.float32)


def softmax_terms(keys, values, query, grad):
    scores = nt_dot(keys, query)
    top = jnp.max(scores, axis=0, keepdims=True)
    expo = jnp.exp2((scores - top) * (SCALE * math.log2(math.e)))
    total = jnp.sum(expo, axis=0, keepdims=True)
    grad_probs = nt_dot(values, grad)
    delta = jnp.sum(expo * grad_probs, axis=0, keepdims=True) / total
    return expo, total, grad_probs, delta


def gather_block(block, place_ref, received, query_cols, grad_cols):
    for lane in range(GROUP):
        place = place_ref[block * GROUP + lane]
        query_cols[lane * 32:lane * 32 + 32] = received[place]
        grad_cols[lane * 32:lane * 32 + 32] = received[place + CAP]


def query_grad_kernel(
    tiles_ref, gate_ref, key_ref, value_ref, turned_ref, received,
    out_ref, place_ref, blocks_ref,
    slot_list, query_cols, grad_cols,
):
    slots = out_ref.shape[0]
    out_ref[...] = jnp.zeros(out_ref.shape, out_ref.dtype)
    found = jnp.int32(0)
    spare = jnp.int32(0)
    for slot in range(slots):
        place = slot // CAP * (2 * CAP) + slot % CAP
        slab = jnp.abs(received[place + CAP].astype(jnp.float32))
        live = jnp.max(slab) > 0.0
        place_ref[found] = jnp.int32(place)
        slot_list[found] = jnp.int32(slot)
        spare = jnp.where(live, spare, slot)
        found = found + jnp.where(live, 1, 0)
    blocks = (found + (GROUP - 1)) // GROUP
    blocks_ref[0] = blocks
    spare_place = spare // CAP * (2 * CAP) + spare % CAP
    for extra in range(GROUP):
        place_ref[found + extra] = spare_place
        slot_list[found + extra] = spare

    def work(live):
        @pl.loop(0, blocks)
        def _(block):
            gather_block(block, place_ref, received, query_cols, grad_cols)
            for start in range(0, GROUP * 32, SUB):
                query = query_cols[start:start + SUB]
                grad = grad_cols[start:start + SUB]
                expo, total, grad_probs, delta = softmax_terms(
                    key_ref[:live], value_ref[:live], query, grad
                )
                weighted = expo * (gate_ref[...] / total)
                score_grad = (weighted * (grad_probs - delta)).astype(jnp.bfloat16)
                turned = nn_dot(turned_ref[:, :live], score_grad) * SCALE
                slabs = turned.T.astype(jnp.bfloat16).reshape(SUB // 32, 32, HEAD)
                for lane in range(SUB // 32):
                    out_ref[slot_list[block * GROUP + start // 32 + lane]] = slabs[lane]

    most = key_ref.shape[0] // TILE
    for count in range(1, most + 1):
        @pl.when(tiles_ref[0] == count)
        def _(count=count):
            work(count * TILE)


def query_grads(tile_counts, gate, key_rows, value_rows, key_turned, received):
    slots = received.shape[0] // 2
    smem = pl.BlockSpec(memory_space=pltpu.SMEM)
    vmem = pl.BlockSpec(memory_space=pltpu.VMEM)
    return pl.pallas_call(
        query_grad_kernel,
        out_shape=(
            jax.ShapeDtypeStruct((slots, 32, HEAD), jnp.bfloat16),
            jax.ShapeDtypeStruct((slots + GROUP,), jnp.int32),
            jax.ShapeDtypeStruct((1,), jnp.int32),
        ),
        in_specs=[smem, vmem, vmem, vmem, vmem, vmem],
        out_specs=(vmem, smem, smem),
        scratch_shapes=[
            pltpu.SMEM((slots + GROUP,), jnp.int32),
            pltpu.VMEM((GROUP * 32, HEAD), jnp.bfloat16),
            pltpu.VMEM((GROUP * 32, HEAD), jnp.bfloat16),
        ],
        compiler_params=pltpu.CompilerParams(vmem_limit_bytes=40 * 2**20),
        name="query_grads",
    )(tile_counts, gate, key_rows, value_rows, key_turned, received)


def image_grad_kernel(
    tiles_ref, place_ref, blocks_ref, gate_ref, key_ref, value_ref, received,
    grad_key_ref, grad_value_ref,
    key_sum, value_sum, query_cols, grad_cols, score_grads, weights,
):
    key_sum[...] = jnp.zeros(key_sum.shape, jnp.float32)
    value_sum[...] = jnp.zeros(value_sum.shape, jnp.float32)

    def work(live):
        @pl.loop(0, blocks_ref[0])
        def _(block):
            gather_block(block, place_ref, received, query_cols, grad_cols)
            for start in range(0, GROUP * 32, SUB):
                part = pl.ds(start, SUB)
                expo, total, grad_probs, delta = softmax_terms(
                    key_ref[:live], value_ref[:live],
                    query_cols[start:start + SUB], grad_cols[start:start + SUB],
                )
                weighted = expo * (gate_ref[...] / total)
                weights[:live, part] = weighted.astype(jnp.bfloat16)
                score_grads[:live, part] = (weighted * (grad_probs - delta)).astype(jnp.bfloat16)
            key_sum[:live] += nn_dot(score_grads[:live], query_cols[...])
            value_sum[:live] += nn_dot(weights[:live], grad_cols[...])

    most = key_ref.shape[0] // TILE
    for count in range(1, most + 1):
        @pl.when(tiles_ref[0] == count)
        def _(count=count):
            work(count * TILE)

    grad_key_ref[...] = (key_sum[...] * SCALE).astype(jnp.bfloat16)
    grad_value_ref[...] = value_sum[...].astype(jnp.bfloat16)


def image_grads(tile_counts, places, blocks, gate, key_rows, value_rows, received):
    keys = key_rows.shape[0]
    cols = GROUP * 32
    smem = pl.BlockSpec(memory_space=pltpu.SMEM)
    vmem = pl.BlockSpec(memory_space=pltpu.VMEM)
    return pl.pallas_call(
        image_grad_kernel,
        out_shape=(
            jax.ShapeDtypeStruct((keys, HEAD), jnp.bfloat16),
            jax.ShapeDtypeStruct((keys, HEAD), jnp.bfloat16),
        ),
        in_specs=[smem, smem, smem, vmem, vmem, vmem, vmem],
        out_specs=(vmem, vmem),
        scratch_shapes=[
            pltpu.VMEM((keys, HEAD), jnp.float32),
            pltpu.VMEM((keys, HEAD), jnp.float32),
            pltpu.VMEM((cols, HEAD), jnp.bfloat16),
            pltpu.VMEM((cols, HEAD), jnp.bfloat16),
            pltpu.VMEM((keys, cols), jnp.bfloat16),
            pltpu.VMEM((keys, cols), jnp.bfloat16),
        ],
        compiler_params=pltpu.CompilerParams(vmem_limit_bytes=40 * 2**20),
        cost_estimate=pl.CostEstimate(
            flops=8 * received.shape[0] * 16 * keys * HEAD,
            bytes_accessed=4 * 2**20,
            transcendentals=received.shape[0] * 16 * keys,
        ),
        name="image_grads",
    )(tile_counts, places, blocks, gate, key_rows, value_rows, received)


def on_device(
    queries, grad_out, image_keys, image_values, gate_logits, tile_counts, owners, text_only
):
    rows, tokens, width = queries.shape
    heads = width // HEAD
    peers = lax.axis_size("dp")

    def slabs(array):
        split = array.reshape(rows, tokens, heads, HEAD).transpose(0, 2, 1, 3)
        return split.reshape(rows, heads * tokens, HEAD)

    send, slot_of = pack(owners[:, 0], text_only, slabs(queries), slabs(grad_out), peers)
    received = lax.all_to_all(send, "dp", split_axis=0, concat_axis=0, tiled=True)
    received = received.reshape(peers * 2 * CAP, heads * tokens, HEAD)
    key_rows, value_rows = image_keys[0], image_values[0]
    gate = jnp.tile(jnp.repeat(jnp.tanh(gate_logits), tokens), SUB // 32)[None]
    grad_slots, places, blocks = query_grads(
        tile_counts, gate, key_rows, value_rows, key_rows.T, received
    )
    returned = lax.all_to_all(
        grad_slots.reshape(peers, CAP, heads * tokens, HEAD),
        "dp", split_axis=0, concat_axis=0, tiled=True,
    )
    grad_key, grad_value = image_grads(
        tile_counts, places, blocks, gate, key_rows, value_rows, received
    )
    grad_rows = unpack(slot_of, returned.reshape(peers * CAP, heads * tokens, HEAD))
    grad_rows = grad_rows.reshape(rows, heads, tokens, HEAD).transpose(0, 2, 1, 3)
    return grad_rows.reshape(rows, tokens, width), grad_key[None], grad_value[None]


def solution(mesh):
    placed = (
        P("dp", None, "tensor"),
        P("dp", None, "tensor"),
        P("dp", None, "tensor"),
        P("dp", None, "tensor"),
        P("tensor"),
        P("dp"),
        P("dp", None),
        P("dp"),
    )
    return jax.shard_map(
        on_device,
        mesh=mesh,
        in_specs=placed,
        out_specs=(P("dp", None, "tensor"), P("dp", None, "tensor"), P("dp", None, "tensor")),
        check_vma=False,
    )
```

time: 268 us -> 178 us (0.66)
  local copies, waits for them, and re-layouts: 41.3 us -> 2.48 us
  waiting for transfers between devices: 142 us -> 105 us
  matrix products: 33.6 us -> 0 us
  Pallas kernels: 0 us -> 27.8 us
  other arithmetic: 15.3 us -> 0 us
  starting transfers between devices: 32.5 us -> 40.9 us
    all_to_all x3 -> x2, waiting for transfers between devices: 142 us -> 105 us  [the longest x1 76.7 us: on_device(): lax.all_to_all(send, 'dp', split_axis=0, concat_axis=0, tiled=True)]
    dot_general x63 -> x0, matrix products: 33.6 us -> none  [the longest x12 7.91 us: attend(): jnp.einsum('ncgd,kcd->cgnk', grad_four, value_three, preferred_element_ty...]
    pallas_call x0 -> x4, Pallas kernels: none -> 27.8 us  [the longest x1 11.6 us: image_grads(): pl.pallas_call(image_grad_kernel, out_shape=(jax.ShapeDtypeStruct((keys,...]
    all_to_all x6 -> x0, local copies, waits for them, and re-layouts: 18.1 us -> none  [the longest x2 8.38 us: on_device(): lax.all_to_all(send_grad, 'dp', split_axis=0, concat_axis=0, tiled=True)]
    dynamic_slice x12 -> x0, local copies, waits for them, and re-layouts: 11.9 us -> none  [one_block(): grad_block = lax.dynamic_slice_in_dim(recv_grad, block_start, slot_block, 0)]
    all_to_all x3 -> x2, starting transfers between devices: 32.5 us -> 40.9 us  [the longest x1 24.1 us: on_device(): lax.all_to_all(grad_slots.reshape(peers, CAP, heads * tokens, HEAD), 'dp'...]
    another operation x13 -> x0, other arithmetic: 6.71 us -> none
    reduce_sum x13 -> x0, other arithmetic: 5.72 us -> none  [the longest x12 4.88 us: attend(): probs = expo_terms / jnp.sum(expo_terms, axis=-1, keepdims=True)]
  transfers between devices with their start and end apart: 3 -> 2, of which waited for: 3 -> 2; matrix products, arithmetic and copies ran while one was open for 2% -> 0% of each run, Pallas kernels for 0% -> 7%
where the time goes in v1:
time: 178 us; the launch traced here: 177 us
  waiting for transfers between devices  105 us (59%)
  starting transfers between devices  40.9 us (23%)
  Pallas kernels  27.8 us (16%)
  local copies, waits for them, and re-layouts  2.48 us (1%)
    all_to_all x1, waiting for transfers between devices, on_device(): lax.all_to_all(send, 'dp', split_axis=0, concat_axis=0, tiled=True)  76.7 us
    all_to_all x1, waiting for transfers between devices, on_device(): lax.all_to_all(grad_slots.reshape(peers, CAP, heads * tokens, HEAD), 'dp'...  28.3 us
    all_to_all x1, starting transfers between devices, on_device(): lax.all_to_all(grad_slots.reshape(peers, CAP, heads * tokens, HEAD), 'dp'...  24.1 us
    all_to_all x1, starting transfers between devices, on_device(): lax.all_to_all(send, 'dp', split_axis=0, concat_axis=0, tiled=True)  16.7 us
    pallas_call x1, Pallas kernels, image_grads(): pl.pallas_call(image_grad_kernel, out_shape=(jax.ShapeDtypeStruct((keys,...  11.6 us
    pallas_call x1, Pallas kernels, query_grads(): pl.pallas_call(query_grad_kernel, out_shape=(jax.ShapeDtypeStruct((slots,...  9.5 us
    pallas_call x1, Pallas kernels, pack(): pl.pallas_call(pack_kernel, out_shape=(jax.ShapeDtypeStruct((peers, 2 * C...  4.05 us
  transfers between devices with their start and end apart: 2, of which 2 were waited for; matrix products, arithmetic and copies ran while one was open for 0% of the time, Pallas kernels for 7%

profile of v1, /device:TPU:6, one launch (start us, length us, event | category | flops | bytes accessed | tf_op | source)
XLA Modules:
  0.0 177.5 jit_solution(14963753869709316450)
XLA Ops:
  0.6 4.1 %pack_rows.1 = (bf16[64,6,32,128]{3,2,1,0:T(8,128)(2,1)}, s32[128]{0:T(128)}) custom-call(s32[128]{0:T(128)} %bitcast.36, s32[128]{0:T(128)} %text_hbm.1, bf16[128,32,128]{2,1,0:T(8,128)(2,1)} %bitcast.34, bf16[128,32,128]{2,1,0:T(8,128)(2,1)} %bitcast.35), custom_call_target="tpu_custom_call" | custom-call | tf_op jit(solution)/shard_map/pack_rows/pallas_call | solution.py:80
  4.7 0.0 copy-start.5
  4.7 0.0 copy-start.1
  4.7 16.7 %all-to-all-start = ((bf16[64,6,32,128]{3,2,1,0:T(8,128)(2,1)}), bf16[64,6,32,128]{3,2,1,0:T(8,128)(2,1)S(1)}, u32[]{:S(2)}, u32[]{:S(2)}) async-start(bf16[64,6,32,128]{3,2,1,0:T(8,128)(2,1)} %get-tuple-element.11), calls=%async_computation | async-start | bytes 6291456 | tf_op jit(solution)/shard_map/all_to_all | solution.py:313
  21.5 0.0 copy-done.5
  21.5 0.1 broadcast_in_dim.9
  21.5 0.1 tile.7
  21.6 0.1 broadcast_in_dim_tile.3.gate_ref
  22.4 0.0 copy-done.1
  22.4 0.1 copy.17.turned_ref
  22.5 76.7 %all-to-all-done = bf16[64,6,32,128]{3,2,1,0:T(8,128)(2,1)S(1)} async-done(((bf16[64,6,32,128]{3,2,1,0:T(8,128)(2,1)}), bf16[64,6,32,128]{3,2,1,0:T(8,128)(2,1)S(1)}, u32[]{:S(2)}, u32[]{:S(2)}) %all-to-all-start) | async-done | bytes 3145760 | tf_op jit(solution)/shard_map/all_to_all | solution.py:313
  99.2 0.0 copy-start.2
  99.2 0.9 copy-done.2
  100.2 9.5 %query_grads.1 = (bf16[192,32,128]{2,1,0:T(8,128)(2,1)S(1)}, s32[208]{0:T(256)S(1)}, s32[1]{0:T(128)}) custom-call(s32[1]{0:T(128)S(6)} %copy.19.tiles_ref, f32[1,256]{1,0:T(1,128)S(1)} %broadcast_in_dim_tile.3.gate_ref, bf16[768,128]{1,0:T(8,128)(2,1)S(1)} %bitcast.29, bf16[768,128]{1,0:T(8,128)(2,1)S(1)} %bitcast.31, ...), custom_call_target="tpu_custom_call" | custom-call | tf_op jit(solution)/shard_map/query_grads/pallas_call | solution.py:217
  109.7 0.0 copy-start
  109.7 1.1 copy-done
  110.8 0.0 copy-start.3
  110.8 24.1 %all-to-all-start.1 = ((bf16[64,3,32,128]{3,2,1,0:T(8,128)(2,1)}), bf16[64,3,32,128]{3,2,1,0:T(8,128)(2,1)}, u32[]{:S(2)}, u32[]{:S(2)}) async-start(bf16[64,3,32,128]{3,2,1,0:T(8,128)(2,1)} %bitcast.27), calls=%async_computation.1 | async-start | bytes 3145728 | tf_op jit(solution)/shard_map/all_to_all | solution.py:320
  135.0 0.0 copy-done.3
  135.0 0.0 copy-start.4
  135.0 11.6 %image_grads.1 = (bf16[768,128]{1,0:T(8,128)(2,1)}, bf16[768,128]{1,0:T(8,128)(2,1)}) custom-call(s32[1]{0:T(128)S(6)} %copy.19.tiles_ref, s32[208]{0:T(256)S(1)} %get-tuple-element.13.place_ref, s32[1]{0:T(128)} %get-tuple-element.14.blocks_ref, f32[1,256]{1,0:T(1,128)S(1)} %broadcast_in_dim_tile.3.gate_ref, bf16[768,128]{1,0:T(8,128)(2,1)S(1)} %bitcast.30, ...), custom_call_target="tpu_custom_call" | custom-call | flops 4831838208 | bytes 4194304 | tf_op jit(solution)/shard_map/image_grads/pallas_call | solution.py:275
  146.5 28.3 %all-to-all-done.1 = bf16[64,3,32,128]{3,2,1,0:T(8,128)(2,1)} async-done(((bf16[64,3,32,128]{3,2,1,0:T(8,128)(2,1)}), bf16[64,3,32,128]{3,2,1,0:T(8,128)(2,1)}, u32[]{:S(2)}, u32[]{:S(2)}) %all-to-all-start.1) | async-done | bytes 1572896 | tf_op jit(solution)/shard_map/all_to_all | solution.py:320
  174.8 0.0 copy-done.4
  174.8 2.6 %unpack_rows.1 = bf16[128,32,128]{2,1,0:T(8,128)(2,1)} custom-call(s32[128]{0:T(128)S(1)} %copy-done.4, bf16[192,32,128]{2,1,0:T(8,128)(2,1)} %bitcast.12.slots_ref), custom_call_target="tpu_custom_call" | custom-call | tf_op jit(solution)/shard_map/unpack_rows/pallas_call | solution.py:129
  (2 shorter events, 0.0 us)
Async XLA Ops:
  4.7 16.8 %copy-start.5 = (f32[8]{0:T(128)S(1)}, f32[8]{0:T(128)}, u32[]{:S(2)}) copy-start(f32[8]{0:T(128)} %param.12) | copy-start | bytes 100
  4.7 17.7 %copy-start.1 = (bf16[1,768,128]{2,1,0:T(8,128)(2,1)S(1)}, bf16[1,768,128]{2,1,0:T(8,128)(2,1)}, u32[]{:S(2)}) copy-start(bf16[1,768,128]{2,1,0:T(8,128)(2,1)} %param.10) | copy-start | bytes 589828
  4.7 94.5 %all-to-all-start = ((bf16[64,6,32,128]{3,2,1,0:T(8,128)(2,1)}), bf16[64,6,32,128]{3,2,1,0:T(8,128)(2,1)S(1)}, u32[]{:S(2)}, u32[]{:S(2)}) async-start(bf16[64,6,32,128]{3,2,1,0:T(8,128)(2,1)} %get-tuple-element.11), calls=%async_computation | async-start | bytes 6291456 | tf_op jit(solution)/shard_map/all_to_all | solution.py:313
  99.2 0.9 copy-start.2
  109.7 1.2 copy-start
  110.8 24.1 %copy-start.3 = (bf16[1,768,128]{2,1,0:T(8,128)(2,1)S(1)}, bf16[1,768,128]{2,1,0:T(8,128)(2,1)}, u32[]{:S(2)}) copy-start(bf16[1,768,128]{2,1,0:T(8,128)(2,1)} %param.11) | copy-start | bytes 589828
  110.8 64.0 %all-to-all-start.1 = ((bf16[64,3,32,128]{3,2,1,0:T(8,128)(2,1)}), bf16[64,3,32,128]{3,2,1,0:T(8,128)(2,1)}, u32[]{:S(2)}, u32[]{:S(2)}) async-start(bf16[64,3,32,128]{3,2,1,0:T(8,128)(2,1)} %bitcast.27), calls=%async_computation.1 | async-start | bytes 3145728 | tf_op jit(solution)/shard_map/all_to_all | solution.py:320
  135.0 39.9 %copy-start.4 = (s32[128]{0:T(128)S(1)}, s32[128]{0:T(128)}, u32[]{:S(2)}) copy-start(s32[128]{0:T(128)} %get-tuple-element.10.slot_ref) | copy-start | bytes 1540

commit v2 on v1

--- a/solution.py
+++ b/solution.py
@@ -12,6 +12,8 @@
 CAP = 3
 SUB = 256
 GROUP = 16
+CHUNK = 128
+PIECES = 4
 SCALE = HEAD ** (-0.5)
 
 
@@ -33,7 +35,7 @@
     for peer in range(peers):
         count[peer] = 0
     query_slots[...] = jnp.zeros(query_slots.shape, query_slots.dtype)
-    grad_slots[...] = jnp.zeros(grad_slots.shape, grad_slots.dtype)
+    grad_slots[...] = jnp.full(grad_slots.shape, jnp.inf, grad_slots.dtype)
     owner_copy.wait()
     text_copy.wait()
 
@@ -145,74 +147,119 @@
     return jnp.dot(a, b, preferred_element_type=jnp.float32)
 
 
-def softmax_terms(keys, values, query, grad):
-    scores = nt_dot(keys, query)
-    top = jnp.max(scores, axis=0, keepdims=True)
-    expo = jnp.exp2((scores - top) * (SCALE * math.log2(math.e)))
-    total = jnp.sum(expo, axis=0, keepdims=True)
-    grad_probs = nt_dot(values, grad)
-    delta = jnp.sum(expo * grad_probs, axis=0, keepdims=True) / total
-    return expo, total, grad_probs, delta
-
-
-def gather_block(block, place_ref, received, query_cols, grad_cols):
+def softmax_terms(key_value_ref, live, query, grad, gate):
+    keys = key_value_ref.shape[0] // 2
+    cols = query.shape[0]
+    scores = nt_dot(key_value_ref[:live], query)
+    grad_probs = nt_dot(key_value_ref[keys:keys + live], grad)
+    tops, expos, grads, sums, dots = [], [], [], [], []
+    for start in range(0, live, CHUNK):
+        score = scores[start:start + CHUNK].reshape(CHUNK // 8, 8, cols)
+        top = jnp.max(score, axis=0)
+        expo = jnp.exp2((score - top) * (SCALE * math.log2(math.e)))
+        grad_prob = grad_probs[start:start + CHUNK].reshape(CHUNK // 8, 8, cols)
+        tops.append(top)
+        expos.append(expo)
+        grads.append(grad_prob)
+        sums.append(jnp.sum(expo, axis=0))
+        dots.append(jnp.sum(expo * grad_prob, axis=0))
+    largest = tops[0]
+    for top in tops[1:]:
+        largest = jnp.maximum(largest, top)
+    largest = jnp.max(largest, axis=0, keepdims=True)
+    factors = [jnp.exp2((top - largest) * (SCALE * math.log2(math.e))) for top in tops]
+    total = sum(factor * part for factor, part in zip(factors, sums))
+    delta = sum(factor * part for factor, part in zip(factors, dots))
+    inverse = 1.0 / jnp.sum(total, axis=0, keepdims=True)
+    delta = jnp.sum(delta, axis=0, keepdims=True) * inverse
+    factors = [factor * (inverse * gate) for factor in factors]
+    return expos, grads, factors, jnp.broadcast_to(delta, (8, cols))
+
+
+def gather_block(block, found, place_ref, received, query_cols, grad_cols):
     for lane in range(GROUP):
-        place = place_ref[block * GROUP + lane]
+        index = block * GROUP + lane
+        place = place_ref[index]
+        grad = received[place + CAP]
         query_cols[lane * 32:lane * 32 + 32] = received[place]
-        grad_cols[lane * 32:lane * 32 + 32] = received[place + CAP]
+        grad_cols[lane * 32:lane * 32 + 32] = jnp.where(index < found, grad, jnp.zeros_like(grad))
 
 
 def query_grad_kernel(
-    tiles_ref, gate_ref, key_ref, value_ref, turned_ref, received,
-    out_ref, place_ref, blocks_ref,
-    slot_list, query_cols, grad_cols,
+    tiles_ref, gate_ref, key_value_hbm, turned_hbm, received_hbm,
+    out_hbm, place_ref, found_ref,
+    slot_list, key_value_ref, turned_ref, received,
+    query_cols, grad_cols, score_grads, out_slots, in_sems, out_sem,
 ):
-    slots = out_ref.shape[0]
-    out_ref[...] = jnp.zeros(out_ref.shape, out_ref.dtype)
+    slots = out_hbm.shape[0]
+    peers = slots // CAP
+    share = received.shape[0] // PIECES
+    in_copies = []
+    for number in range(PIECES):
+        piece = pl.ds(number * share, share)
+        in_copies.append(pltpu.make_async_copy(
+            received_hbm.at[piece], received.at[piece], in_sems.at[number]
+        ))
+    key_copy = pltpu.make_async_copy(key_value_hbm, key_value_ref, in_sems.at[PIECES])
+    turned_copy = pltpu.make_async_copy(turned_hbm, turned_ref, in_sems.at[PIECES + 1])
+    for copy in in_copies:
+        copy.start()
+    key_copy.start()
+    turned_copy.start()
     found = jnp.int32(0)
-    spare = jnp.int32(0)
-    for slot in range(slots):
-        place = slot // CAP * (2 * CAP) + slot % CAP
-        slab = jnp.abs(received[place + CAP].astype(jnp.float32))
-        live = jnp.max(slab) > 0.0
-        place_ref[found] = jnp.int32(place)
-        slot_list[found] = jnp.int32(slot)
-        spare = jnp.where(live, spare, slot)
-        found = found + jnp.where(live, 1, 0)
-    blocks = (found + (GROUP - 1)) // GROUP
-    blocks_ref[0] = blocks
-    spare_place = spare // CAP * (2 * CAP) + spare % CAP
+    for peer in range(peers):
+        if peer % (peers // PIECES) == 0:
+            in_copies[peer // (peers // PIECES)].wait()
+        used = jnp.zeros((16, HEAD), jnp.float32)
+        for rank in range(CAP):
+            first = received[peer * 2 * CAP + CAP + rank, 0:16].astype(jnp.float32)
+            used = used + jnp.where(first < jnp.inf, 1.0, 0.0)
+            place_ref[found + rank] = jnp.int32(peer * 2 * CAP + rank)
+            slot_list[found + rank] = jnp.int32(peer * CAP + rank)
+        found = found + used[0, 0].astype(jnp.int32)
+    found_ref[0] = found
     for extra in range(GROUP):
-        place_ref[found + extra] = spare_place
-        slot_list[found + extra] = spare
+        place_ref[found + extra] = jnp.int32(0)
+        slot_list[found + extra] = jnp.int32(slots)
+    key_copy.wait()
+    turned_copy.wait()
 
     def work(live):
-        @pl.loop(0, blocks)
+        @pl.loop(0, (found + (GROUP - 1)) // GROUP)
         def _(block):
-            gather_block(block, place_ref, received, query_cols, grad_cols)
+            gather_block(block, found, place_ref, received, query_cols, grad_cols)
             for start in range(0, GROUP * 32, SUB):
-                query = query_cols[start:start + SUB]
-                grad = grad_cols[start:start + SUB]
-                expo, total, grad_probs, delta = softmax_terms(
-                    key_ref[:live], value_ref[:live], query, grad
+                expos, grads, factors, delta = softmax_terms(
+                    key_value_ref, live,
+                    query_cols[start:start + SUB], grad_cols[start:start + SUB], gate_ref[...],
                 )
-                weighted = expo * (gate_ref[...] / total)
-                score_grad = (weighted * (grad_probs - delta)).astype(jnp.bfloat16)
-                turned = nn_dot(turned_ref[:, :live], score_grad) * SCALE
-                slabs = turned.T.astype(jnp.bfloat16).reshape(SUB // 32, 32, HEAD)
+                for number, (expo, grad, factor) in enumerate(zip(expos, grads, factors)):
+                    score_grad = expo * factor * (grad - delta)
+                    score_grads[number * CHUNK:(number + 1) * CHUNK, start:start + SUB] = (
+                        score_grad.reshape(CHUNK, SUB).astype(jnp.bfloat16)
+                    )
+                turned = nn_dot(turned_ref[:, :live], score_grads[:live, start:start + SUB])
+                slabs = (turned * SCALE).T.astype(jnp.bfloat16).reshape(SUB // 32, 32, HEAD)
                 for lane in range(SUB // 32):
-                    out_ref[slot_list[block * GROUP + start // 32 + lane]] = slabs[lane]
-
-    most = key_ref.shape[0] // TILE
+                    out_slots[slot_list[block * GROUP + start // 32 + lane]] = slabs[lane]
+
+    most = key_value_ref.shape[0] // 2 // TILE
     for count in range(1, most + 1):
         @pl.when(tiles_ref[0] == count)
         def _(count=count):
             work(count * TILE)
 
-
-def query_grads(tile_counts, gate, key_rows, value_rows, key_turned, received):
+    out = pltpu.make_async_copy(out_slots.at[pl.ds(0, slots)], out_hbm, out_sem)
+    out.start()
+    out.wait()
+
+
+def query_grads(tile_counts, gate, key_values, key_turned, received):
     slots = received.shape[0] // 2
+    keys = key_values.shape[0] // 2
+    cols = GROUP * 32
     smem = pl.BlockSpec(memory_space=pltpu.SMEM)
+    hbm = pl.BlockSpec(memory_space=pltpu.HBM)
     vmem = pl.BlockSpec(memory_space=pltpu.VMEM)
     return pl.pallas_call(
         query_grad_kernel,
@@ -221,43 +268,57 @@
             jax.ShapeDtypeStruct((slots + GROUP,), jnp.int32),
             jax.ShapeDtypeStruct((1,), jnp.int32),
         ),
-        in_specs=[smem, vmem, vmem, vmem, vmem, vmem],
-        out_specs=(vmem, smem, smem),
+        in_specs=[smem, vmem, hbm, hbm, hbm],
+        out_specs=(hbm, smem, smem),
         scratch_shapes=[
             pltpu.SMEM((slots + GROUP,), jnp.int32),
-            pltpu.VMEM((GROUP * 32, HEAD), jnp.bfloat16),
-            pltpu.VMEM((GROUP * 32, HEAD), jnp.bfloat16),
+            pltpu.VMEM(key_values.shape, jnp.bfloat16),
+            pltpu.VMEM(key_turned.shape, jnp.bfloat16),
+            pltpu.VMEM(received.shape, jnp.bfloat16),
+            pltpu.VMEM((cols, HEAD), jnp.bfloat16),
+            pltpu.VMEM((cols, HEAD), jnp.bfloat16),
+            pltpu.VMEM((keys, cols), jnp.bfloat16),
+            pltpu.VMEM((slots + 1, 32, HEAD), jnp.bfloat16),
+            pltpu.SemaphoreType.DMA((PIECES + 2,)),
+            pltpu.SemaphoreType.DMA,
         ],
-        compiler_params=pltpu.CompilerParams(vmem_limit_bytes=40 * 2**20),
+        compiler_params=pltpu.CompilerParams(vmem_limit_bytes=60 * 2**20),
         name="query_grads",
-    )(tile_counts, gate, key_rows, value_rows, key_turned, received)
+    )(tile_counts, gate, key_values, key_turned, received)
 
 
 def image_grad_kernel(
-    tiles_ref, place_ref, blocks_ref, gate_ref, key_ref, value_ref, received,
+    tiles_ref, place_ref, found_ref, gate_ref, key_value_ref, received,
     grad_key_ref, grad_value_ref,
     key_sum, value_sum, query_cols, grad_cols, score_grads, weights,
 ):
+    found = found_ref[0]
     key_sum[...] = jnp.zeros(key_sum.shape, jnp.float32)
     value_sum[...] = jnp.zeros(value_sum.shape, jnp.float32)
 
     def work(live):
-        @pl.loop(0, blocks_ref[0])
+        @pl.loop(0, (found + (GROUP - 1)) // GROUP)
         def _(block):
-            gather_block(block, place_ref, received, query_cols, grad_cols)
+            gather_block(block, found, place_ref, received, query_cols, grad_cols)
             for start in range(0, GROUP * 32, SUB):
-                part = pl.ds(start, SUB)
-                expo, total, grad_probs, delta = softmax_terms(
-                    key_ref[:live], value_ref[:live],
-                    query_cols[start:start + SUB], grad_cols[start:start + SUB],
+                expos, grads, factors, delta = softmax_terms(
+                    key_value_ref, live,
+                    query_cols[start:start + SUB], grad_cols[start:start + SUB], gate_ref[...],
                 )
-                weighted = expo * (gate_ref[...] / total)
-                weights[:live, part] = weighted.astype(jnp.bfloat16)
-                score_grads[:live, part] = (weighted * (grad_probs - delta)).astype(jnp.bfloat16)
+                for number, (expo, grad, factor) in enumerate(zip(expos, grads, factors)):
+                    rows = slice(number * CHUNK, (number + 1) * CHUNK)
+                    weighted = expo * factor
+                    score_grad = weighted * (grad - delta)
+                    weights[rows, start:start + SUB] = (
+                        weighted.reshape(CHUNK, SUB).astype(jnp.bfloat16)
+                    )
+                    score_grads[rows, start:start + SUB] = (
+                        score_grad.reshape(CHUNK, SUB).astype(jnp.bfloat16)
+                    )
             key_sum[:live] += nn_dot(score_grads[:live], query_cols[...])
             value_sum[:live] += nn_dot(weights[:live], grad_cols[...])
 
-    most = key_ref.shape[0] // TILE
+    most = key_value_ref.shape[0] // 2 // TILE
     for count in range(1, most + 1):
         @pl.when(tiles_ref[0] == count)
         def _(count=count):
@@ -267,8 +328,8 @@
     grad_value_ref[...] = value_sum[...].astype(jnp.bfloat16)
 
 
-def image_grads(tile_counts, places, blocks, gate, key_rows, value_rows, received):
-    keys = key_rows.shape[0]
+def image_grads(tile_counts, places, found, gate, key_values, received):
+    keys = key_values.shape[0] // 2
     cols = GROUP * 32
     smem = pl.BlockSpec(memory_space=pltpu.SMEM)
     vmem = pl.BlockSpec(memory_space=pltpu.VMEM)
@@ -278,7 +339,7 @@
             jax.ShapeDtypeStruct((keys, HEAD), jnp.bfloat16),
             jax.ShapeDtypeStruct((keys, HEAD), jnp.bfloat16),
         ),
-        in_specs=[smem, smem, smem, vmem, vmem, vmem, vmem],
+        in_specs=[smem, smem, smem, vmem, vmem, vmem],
         out_specs=(vmem, vmem),
         scratch_shapes=[
             pltpu.VMEM((keys, HEAD), jnp.float32),
@@ -295,7 +356,7 @@
             transcendentals=received.shape[0] * 16 * keys,
         ),
         name="image_grads",
-    )(tile_counts, places, blocks, gate, key_rows, value_rows, received)
+    )(tile_counts, places, found, gate, key_values, received)
 
 
 def on_device(
@@ -312,18 +373,16 @@
     send, slot_of = pack(owners[:, 0], text_only, slabs(queries), slabs(grad_out), peers)
     received = lax.all_to_all(send, "dp", split_axis=0, concat_axis=0, tiled=True)
     received = received.reshape(peers * 2 * CAP, heads * tokens, HEAD)
-    key_rows, value_rows = image_keys[0], image_values[0]
+    key_values = jnp.concatenate([image_keys[0], image_values[0]])
     gate = jnp.tile(jnp.repeat(jnp.tanh(gate_logits), tokens), SUB // 32)[None]
-    grad_slots, places, blocks = query_grads(
-        tile_counts, gate, key_rows, value_rows, key_rows.T, received
+    grad_slots, places, found = query_grads(
+        tile_counts, gate, key_values, image_keys[0].T, received
     )
     returned = lax.all_to_all(
         grad_slots.reshape(peers, CAP, heads * tokens, HEAD),
         "dp", split_axis=0, concat_axis=0, tiled=True,
     )
-    grad_key, grad_value = image_grads(
-        tile_counts, places, blocks, gate, key_rows, value_rows, received
-    )
+    grad_key, grad_value = image_grads(tile_counts, places, found, gate, key_values, received)
     grad_rows = unpack(slot_of, returned.reshape(peers * CAP, heads * tokens, HEAD))
     grad_rows = grad_rows.reshape(rows, heads, tokens, HEAD).transpose(0, 2, 1, 3)
     return grad_rows.reshape(rows, tokens, width), grad_key[None], grad_value[None]

time: 178 us -> 180 us (1.011)
  Pallas kernels: 27.8 us -> 29.8 us
    pallas_call x1, Pallas kernels: 9.5 us -> 13 us  [query_grads(): pl.pallas_call(query_grad_kernel, out_shape=(jax.ShapeDtypeStruct((slots,...]
    all_to_all x1, waiting for transfers between devices: 76.7 us -> 74.7 us  [on_device(): lax.all_to_all(send, 'dp', split_axis=0, concat_axis=0, tiled=True)]
  transfers between devices with their start and end apart: 2 -> 2, of which waited for: 2 -> 2; matrix products, arithmetic and copies ran while one was open for 0% -> 1% of each run, Pallas kernels for 7% -> 6%
where the time goes in v2:
time: 180 us
  waiting for transfers between devices  104 us (58%)
  starting transfers between devices  40.1 us (22%)
  Pallas kernels  29.8 us (17%)
  local copies, waits for them, and re-layouts  3.31 us (2%)
    all_to_all x1, waiting for transfers between devices, on_device(): lax.all_to_all(send, 'dp', split_axis=0, concat_axis=0, tiled=True)  74.7 us
    all_to_all x1, waiting for transfers between devices, on_device(): lax.all_to_all(grad_slots.reshape(peers, CAP, heads * tokens, HEAD), 'dp'...  29.7 us
    all_to_all x1, starting transfers between devices, on_device(): lax.all_to_all(grad_slots.reshape(peers, CAP, heads * tokens, HEAD), 'dp'...  23.3 us
    all_to_all x1, starting transfers between devices, on_device(): lax.all_to_all(send, 'dp', split_axis=0, concat_axis=0, tiled=True)  16.7 us
    pallas_call x1, Pallas kernels, query_grads(): pl.pallas_call(query_grad_kernel, out_shape=(jax.ShapeDtypeStruct((slots,...  13 us
    pallas_call x1, Pallas kernels, image_grads(): pl.pallas_call(image_grad_kernel, out_shape=(jax.ShapeDtypeStruct((keys,...  10.1 us
    pallas_call x1, Pallas kernels, pack(): pl.pallas_call(pack_kernel, out_shape=(jax.ShapeDtypeStruct((peers, 2 * C...  4.05 us
  transfers between devices with their start and end apart: 2, of which 2 were waited for; matrix products, arithmetic and copies ran while one was open for 1% of the time, Pallas kernels for 6%

profile of v2, /device:TPU:6, one launch (start us, length us, event | category | flops | bytes accessed | tf_op | source)
XLA Modules:
  0.0 179.8 jit_solution(435573816449250165)
XLA Ops:
  0.6 4.0 %pack_rows.1 = (bf16[64,6,32,128]{3,2,1,0:T(8,128)(2,1)}, s32[128]{0:T(128)}) custom-call(s32[128]{0:T(128)} %bitcast.34, s32[128]{0:T(128)} %text_hbm.1, bf16[128,32,128]{2,1,0:T(8,128)(2,1)} %bitcast.29, bf16[128,32,128]{2,1,0:T(8,128)(2,1)} %bitcast.30), custom_call_target="tpu_custom_call" | custom-call | tf_op jit(solution)/shard_map/pack_rows/pallas_call | solution.py:82
  4.7 0.0 copy-start.8
  4.7 0.0 copy-start.6
  4.7 0.0 copy-start.7
  4.7 16.7 %all-to-all-start = ((bf16[64,6,32,128]{3,2,1,0:T(8,128)(2,1)}), bf16[64,6,32,128]{3,2,1,0:T(8,128)(2,1)S(1)}, u32[]{:S(2)}, u32[]{:S(2)}) async-start(bf16[64,6,32,128]{3,2,1,0:T(8,128)(2,1)} %get-tuple-element.11), calls=%async_computation | async-start | bytes 6291456 | tf_op jit(solution)/shard_map/all_to_all | solution.py:374
  21.5 0.0 copy-done.8
  21.5 0.1 broadcast_in_dim.9
  21.6 0.1 tile.7
  21.6 0.6 broadcast_in_dim_tile.3.gate_ref
  22.9 0.0 copy-done.6
  22.9 0.8 copy.17.turned_hbm
  23.8 0.0 copy-done.7
  23.8 0.8 pad_maximum_fusion.key_value_hbm.key_value_ref
  24.5 74.7 %all-to-all-done = bf16[64,6,32,128]{3,2,1,0:T(8,128)(2,1)S(1)} async-done(((bf16[64,6,32,128]{3,2,1,0:T(8,128)(2,1)}), bf16[64,6,32,128]{3,2,1,0:T(8,128)(2,1)S(1)}, u32[]{:S(2)}, u32[]{:S(2)}) %all-to-all-start) | async-done | bytes 3145760 | tf_op jit(solution)/shard_map/all_to_all | solution.py:374
  99.2 0.0 copy-start
  99.2 1.6 copy-done
  100.9 0.0 copy-start.2
  100.9 0.0 copy-start.3
  100.9 13.0 %query_grads.1 = (bf16[192,32,128]{2,1,0:T(8,128)(2,1)}, s32[208]{0:T(256)}, s32[1]{0:T(128)}) custom-call(s32[1]{0:T(128)S(6)} %copy.19.tiles_ref, f32[1,256]{1,0:T(1,128)} %broadcast_in_dim_tile.3.gate_ref, bf16[1536,128]{1,0:T(8,128)(2,1)} %pad_maximum_fusion.key_value_hbm.key_value_ref, bf16[128,768]{1,0:T(8,128)(2,1)} %copy.17.turned_hbm, ...), custom_call_target="tpu_custom_call" | custom-call | tf_op jit(solution)/shard_map/query_grads/pallas_call | solution.py:264
  113.9 0.0 copy-start.1
  113.9 0.0 copy-start.5
  113.9 23.3 %all-to-all-start.1 = ((bf16[64,3,32,128]{3,2,1,0:T(8,128)(2,1)}), bf16[64,3,32,128]{3,2,1,0:T(8,128)(2,1)}, u32[]{:S(2)}, u32[]{:S(2)}) async-start(bf16[64,3,32,128]{3,2,1,0:T(8,128)(2,1)} %bitcast.27), calls=%async_computation.1 | async-start | bytes 3145728 | tf_op jit(solution)/shard_map/all_to_all | solution.py:381
  137.3 0.0 copy-done.2
  137.3 0.0 copy-done.3
  137.3 0.0 copy-done.1
  137.3 0.0 copy-done.5
  137.3 0.0 copy-start.4
  137.3 10.1 %image_grads.1 = (bf16[768,128]{1,0:T(8,128)(2,1)}, bf16[768,128]{1,0:T(8,128)(2,1)}) custom-call(s32[1]{0:T(128)S(6)} %copy.19.tiles_ref, s32[208]{0:T(256)S(1)} %copy-done.5, s32[1]{0:T(128)} %get-tuple-element.14.found_ref, f32[1,256]{1,0:T(1,128)S(1)} %copy-done.3, bf16[1536,128]{1,0:T(8,128)(2,1)S(1)} %copy-done.2, bf16[384,32,128]{2,1,0:T(8,128)(2,1)S(1)} %bitcast.26), custom_call_target="tpu_custom_call" | custom-call | flops 4831838208 | bytes 4194304 | tf_op jit(solution)/shard_map/image_grads/pallas_call | solution.py:336
  147.5 29.7 %all-to-all-done.1 = bf16[64,3,32,128]{3,2,1,0:T(8,128)(2,1)} async-done(((bf16[64,3,32,128]{3,2,1,0:T(8,128)(2,1)}), bf16[64,3,32,128]{3,2,1,0:T(8,128)(2,1)}, u32[]{:S(2)}, u32[]{:S(2)}) %all-to-all-start.1) | async-done | bytes 1572896 | tf_op jit(solution)/shard_map/all_to_all | solution.py:381
  177.1 0.0 copy-done.4
  177.1 2.6 %unpack_rows.1 = bf16[128,32,128]{2,1,0:T(8,128)(2,1)} custom-call(s32[128]{0:T(128)S(1)} %copy-done.4, bf16[192,32,128]{2,1,0:T(8,128)(2,1)} %bitcast.12.slots_ref), custom_call_target="tpu_custom_call" | custom-call | tf_op jit(solution)/shard_map/unpack_rows/pallas_call | solution.py:131
  (2 shorter events, 0.0 us)
Async XLA Ops:
  4.7 16.8 %copy-start.8 = (f32[8]{0:T(128)S(1)}, f32[8]{0:T(128)}, u32[]{:S(2)}) copy-start(f32[8]{0:T(128)} %param.12) | copy-start | bytes 100
  4.7 18.2 %copy-start.6 = (bf16[1,768,128]{2,1,0:T(8,128)(2,1)S(1)}, bf16[1,768,128]{2,1,0:T(8,128)(2,1)}, u32[]{:S(2)}) copy-start(bf16[1,768,128]{2,1,0:T(8,128)(2,1)} %param.10) | copy-start | bytes 589828
  4.7 19.1 %copy-start.7 = (bf16[1,768,128]{2,1,0:T(8,128)(2,1)S(1)}, bf16[1,768,128]{2,1,0:T(8,128)(2,1)}, u32[]{:S(2)}) copy-start(bf16[1,768,128]{2,1,0:T(8,128)(2,1)} %param.11) | copy-start | bytes 589828
  4.7 94.5 %all-to-all-start = ((bf16[64,6,32,128]{3,2,1,0:T(8,128)(2,1)}), bf16[64,6,32,128]{3,2,1,0:T(8,128)(2,1)S(1)}, u32[]{:S(2)}, u32[]{:S(2)}) async-start(bf16[64,6,32,128]{3,2,1,0:T(8,128)(2,1)} %get-tuple-element.11), calls=%async_computation | async-start | bytes 6291456 | tf_op jit(solution)/shard_map/all_to_all | solution.py:374
  99.2 1.6 copy-start
  100.9 36.4 %copy-start.2 = (bf16[1536,128]{1,0:T(8,128)(2,1)S(1)}, bf16[1536,128]{1,0:T(8,128)(2,1)}, u32[]{:S(2)}) copy-start(bf16[1536,128]{1,0:T(8,128)(2,1)} %pad_maximum_fusion.key_value_hbm.key_value_ref) | copy-start | bytes 1179652
  100.9 36.4 %copy-start.3 = (f32[1,256]{1,0:T(1,128)S(1)}, f32[1,256]{1,0:T(1,128)}, u32[]{:S(2)}) copy-start(f32[1,256]{1,0:T(1,128)} %broadcast_in_dim_tile.3.gate_ref) | copy-start | bytes 3076
  113.9 23.4 %copy-start.1 = (bf16[64,6,32,128]{3,2,1,0:T(8,128)(2,1)S(1)}, bf16[64,6,32,128]{3,2,1,0:T(8,128)(2,1)}, u32[]{:S(2)}) copy-start(bf16[64,6,32,128]{3,2,1,0:T(8,128)(2,1)} %copy-done) | copy-start | bytes 9437188
  113.9 23.4 %copy-start.5 = (s32[208]{0:T(256)S(1)}, s32[208]{0:T(256)}, u32[]{:S(2)}) copy-start(s32[208]{0:T(256)} %get-tuple-element.13.place_ref) | copy-start | bytes 2500
  113.9 63.2 %all-to-all-start.1 = ((bf16[64,3,32,128]{3,2,1,0:T(8,128)(2,1)}), bf16[64,3,32,128]{3,2,1,0:T(8,128)(2,1)}, u32[]{:S(2)}, u32[]{:S(2)}) async-start(bf16[64,3,32,128]{3,2,1,0:T(8,128)(2,1)} %bitcast.27), calls=%async_computation.1 | async-start | bytes 3145728 | tf_op jit(solution)/shard_map/all_to_all | solution.py:381
  137.3 39.8 %copy-start.4 = (s32[128]{0:T(128)S(1)}, s32[128]{0:T(128)}, u32[]{:S(2)}) copy-start(s32[128]{0:T(128)} %get-tuple-element.10.slot_ref) | copy-start | bytes 1540

commit v3 on v2

v3 whole, which is shorter than its diff:
```python
import math

import jax
import jax.numpy as jnp
from jax import lax
from jax.experimental import pallas as pl
from jax.experimental.pallas import tpu as pltpu
from jax.sharding import PartitionSpec as P

HEAD = 128
TILE = 256
CAP = 3
SUB = 256
GROUP = 16
DEPTH = 16
HALVES = 2
CHUNK = 128
SCALE = HEAD ** (-0.5)


def pack_kernel(
    owner_hbm, text_hbm, query_hbm, grad_hbm, send_first, send_second, slot_ref,
    owners, texts, count, place_of, query_rows, grad_rows, query_slots, grad_slots,
    in_sems, out_sems,
):
    rows = query_rows.shape[0]
    peers = query_slots.shape[0] - 1
    send_refs = (send_first, send_second)
    owner_copy = pltpu.make_async_copy(owner_hbm, owners, in_sems.at[0])
    text_copy = pltpu.make_async_copy(text_hbm, texts, in_sems.at[1])
    query_copy = pltpu.make_async_copy(query_hbm, query_rows, in_sems.at[2])
    grad_copy = pltpu.make_async_copy(grad_hbm, grad_rows, in_sems.at[3])
    owner_copy.start()
    text_copy.start()
    query_copy.start()
    grad_copy.start()
    for peer in range(peers):
        count[peer] = 0
    query_slots[...] = jnp.zeros(query_slots.shape, query_slots.dtype)
    grad_slots[...] = jnp.full(grad_slots.shape, jnp.inf, grad_slots.dtype)
    owner_copy.wait()
    text_copy.wait()

    @pl.loop(0, rows // 8)
    def _(group):
        for inner in range(8):
            row = group * 8 + inner
            owner = owners[row]
            live = texts[row] == 0
            rank = count[owner]
            count[owner] = rank + jnp.where(live, 1, 0)
            place_of[row] = jnp.where(live, owner * 4 + rank, peers * 4)
            slot_ref[row] = jnp.where(live, owner * CAP + rank, -1)

    out_copies = []
    for which, (copy, source, target) in enumerate(
        ((query_copy, query_rows, query_slots), (grad_copy, grad_rows, grad_slots))
    ):
        copy.wait()

        @pl.loop(0, rows // 8)
        def _(group, source=source, target=target):
            for inner in range(8):
                row = group * 8 + inner
                place = place_of[row]
                target[place >> 2, place & 3] = source[row]

        for half, send in enumerate(send_refs):
            out = pltpu.make_async_copy(
                target.at[pl.ds(0, peers), :, pl.ds(half * DEPTH, DEPTH)],
                send.at[:, pl.ds(which * CAP, CAP)],
                out_sems.at[which * HALVES + half],
            )
            out.start()
            out_copies.append(out)
    for out in out_copies:
        out.wait()


def pack(owners, text_only, queries, grad_out, peers):
    rows = queries.shape[0]
    slab = queries.shape[1:]
    hbm = pl.BlockSpec(memory_space=pltpu.HBM)
    padded = (peers + 1, CAP) + slab
    return pl.pallas_call(
        pack_kernel,
        out_shape=(
            jax.ShapeDtypeStruct((peers, 2 * CAP, DEPTH, HEAD), jnp.bfloat16),
            jax.ShapeDtypeStruct((peers, 2 * CAP, DEPTH, HEAD), jnp.bfloat16),
            jax.ShapeDtypeStruct((rows,), jnp.int32),
        ),
        in_specs=[hbm, hbm, hbm, hbm],
        out_specs=(hbm, hbm, pl.BlockSpec(memory_space=pltpu.SMEM)),
        scratch_shapes=[
            pltpu.SMEM((rows,), jnp.int32),
            pltpu.SMEM((rows,), jnp.int32),
            pltpu.SMEM((peers,), jnp.int32),
            pltpu.SMEM((rows,), jnp.int32),
            pltpu.VMEM((rows,) + slab, jnp.bfloat16),
            pltpu.VMEM((rows,) + slab, jnp.bfloat16),
            pltpu.VMEM(padded, jnp.bfloat16),
            pltpu.VMEM(padded, jnp.bfloat16),
            pltpu.SemaphoreType.DMA((4,)),
            pltpu.SemaphoreType.DMA((2 * HALVES,)),
        ],
        compiler_params=pltpu.CompilerParams(vmem_limit_bytes=60 * 2**20),
        name="pack_rows",
    )(owners, text_only, queries, grad_out)


def unpack_kernel(slot_ref, first_ref, second_ref, out_hbm, rows_ref, sems):
    rows = rows_ref.shape[0]
    parts = sems.shape[0]
    share = rows // parts
    copies = []
    for part in range(parts):
        @pl.loop(0, share // 8)
        def _(group, part=part):
            for inner in range(8):
                row = part * share + group * 8 + inner
                slot = slot_ref[row]
                for half, slots_ref in enumerate((first_ref, second_ref)):
                    slab = slots_ref[jnp.maximum(slot, 0)]
                    rows_ref[row, half * DEPTH:(half + 1) * DEPTH] = jnp.where(
                        slot >= 0, slab, jnp.zeros_like(slab)
                    )

        piece = pl.ds(part * share, share)
        copy = pltpu.make_async_copy(rows_ref.at[piece], out_hbm.at[piece], sems.at[part])
        copy.start()
        copies.append(copy)
    for copy in copies:
        copy.wait()


def unpack(slot_of, first, second):
    rows = (slot_of.shape[0], HALVES * DEPTH, HEAD)
    vmem = pl.BlockSpec(memory_space=pltpu.VMEM)
    return pl.pallas_call(
        unpack_kernel,
        out_shape=jax.ShapeDtypeStruct(rows, jnp.bfloat16),
        in_specs=[pl.BlockSpec(memory_space=pltpu.SMEM), vmem, vmem],
        out_specs=pl.BlockSpec(memory_space=pltpu.HBM),
        scratch_shapes=[pltpu.VMEM(rows, jnp.bfloat16), pltpu.SemaphoreType.DMA((4,))],
        compiler_params=pltpu.CompilerParams(vmem_limit_bytes=16 * 2**20),
        name="unpack_rows",
    )(slot_of, first, second)


def nt_dot(a, b):
    return lax.dot_general(a, b, (((1,), (1,)), ((), ())), preferred_element_type=jnp.float32)


def nn_dot(a, b):
    return jnp.dot(a, b, preferred_element_type=jnp.float32)


def softmax_terms(key_value_ref, live, query, grad, gate):
    keys = key_value_ref.shape[0] // 2
    cols = query.shape[0]
    scores = nt_dot(key_value_ref[:live], query)
    grad_probs = nt_dot(key_value_ref[keys:keys + live], grad)
    tops, expos, grads, sums, dots = [], [], [], [], []
    for start in range(0, live, CHUNK):
        score = scores[start:start + CHUNK].reshape(CHUNK // 8, 8, cols)
        top = jnp.max(score, axis=0)
        expo = jnp.exp2((score - top) * (SCALE * math.log2(math.e)))
        grad_prob = grad_probs[start:start + CHUNK].reshape(CHUNK // 8, 8, cols)
        tops.append(top)
        expos.append(expo)
        grads.append(grad_prob)
        sums.append(jnp.sum(expo, axis=0))
        dots.append(jnp.sum(expo * grad_prob, axis=0))
    largest = tops[0]
    for top in tops[1:]:
        largest = jnp.maximum(largest, top)
    largest = jnp.max(largest, axis=0, keepdims=True)
    factors = [jnp.exp2((top - largest) * (SCALE * math.log2(math.e))) for top in tops]
    total = sum(factor * part for factor, part in zip(factors, sums))
    delta = sum(factor * part for factor, part in zip(factors, dots))
    inverse = 1.0 / jnp.sum(total, axis=0, keepdims=True)
    delta = jnp.sum(delta, axis=0, keepdims=True) * inverse
    factors = [factor * (inverse * gate) for factor in factors]
    return expos, grads, factors, jnp.broadcast_to(delta, (8, cols))


def find_slots(received, place_list, slot_list):
    peers = received.shape[0] // (2 * CAP)
    found = jnp.int32(0)
    spare = jnp.int32(0)
    for peer in range(peers):
        used = jnp.zeros((16, HEAD), jnp.float32)
        for rank in range(CAP):
            first = received[peer * 2 * CAP + CAP + rank, 0:16].astype(jnp.float32)
            used = used + jnp.where(first < jnp.inf, 1.0, 0.0)
            place_list[found + rank] = jnp.int32(peer * 2 * CAP + rank)
            slot_list[found + rank] = jnp.int32(peer * CAP + rank)
        count = used[0, 0].astype(jnp.int32)
        spare = jnp.where(count < CAP, jnp.int32(peer), spare)
        found = found + count
    for extra in range(GROUP):
        place_list[found + extra] = spare * (2 * CAP) + (CAP - 1)
        slot_list[found + extra] = spare * CAP + (CAP - 1)
    return found


def gather_block(block, found, place_list, received, query_cols, grad_cols, start):
    for lane in range(GROUP):
        index = block * GROUP + lane
        place = place_list[index]
        grad = received[place + CAP]
        at = start + lane * DEPTH
        query_cols[at:at + DEPTH] = received[place]
        grad_cols[at:at + DEPTH] = jnp.where(index < found, grad, jnp.zeros_like(grad))


def query_grad_kernel(
    tiles_ref, gate_ref, key_value_ref, turned_ref, received, out_ref,
    place_list, slot_list, query_cols, grad_cols, score_grads,
):
    found = find_slots(received, place_list, slot_list)

    def work(live):
        @pl.loop(0, (found + (GROUP - 1)) // GROUP)
        def _(block):
            gather_block(block, found, place_list, received, query_cols, grad_cols, 0)
            for start in range(0, GROUP * DEPTH, SUB):
                expos, grads, factors, delta = softmax_terms(
                    key_value_ref, live,
                    query_cols[start:start + SUB], grad_cols[start:start + SUB], gate_ref[...],
                )
                for number, (expo, grad, factor) in enumerate(zip(expos, grads, factors)):
                    score_grad = expo * factor * (grad - delta)
                    score_grads[number * CHUNK:(number + 1) * CHUNK, start:start + SUB] = (
                        score_grad.reshape(CHUNK, SUB).astype(jnp.bfloat16)
                    )
                turned = nn_dot(turned_ref[:, :live], score_grads[:live, start:start + SUB])
                slabs = (turned * SCALE).T.astype(jnp.bfloat16).reshape(SUB // DEPTH, DEPTH, HEAD)
                for lane in range(SUB // DEPTH):
                    out_ref[slot_list[block * GROUP + start // DEPTH + lane]] = slabs[lane]

    most = key_value_ref.shape[0] // 2 // TILE
    for count in range(1, most + 1):
        @pl.when(tiles_ref[0] == count)
        def _(count=count):
            work(count * TILE)


def query_grads(tile_counts, gate, key_values, key_turned, received):
    slots = received.shape[0] // 2
    keys = key_values.shape[0] // 2
    cols = GROUP * DEPTH
    smem = pl.BlockSpec(memory_space=pltpu.SMEM)
    vmem = pl.BlockSpec(memory_space=pltpu.VMEM)
    return pl.pallas_call(
        query_grad_kernel,
        out_shape=jax.ShapeDtypeStruct((slots, DEPTH, HEAD), jnp.bfloat16),
        in_specs=[smem, vmem, vmem, vmem, vmem],
        out_specs=vmem,
        scratch_shapes=[
            pltpu.SMEM((slots + GROUP,), jnp.int32),
            pltpu.SMEM((slots + GROUP,), jnp.int32),
            pltpu.VMEM((cols, HEAD), jnp.bfloat16),
            pltpu.VMEM((cols, HEAD), jnp.bfloat16),
            pltpu.VMEM((keys, cols), jnp.bfloat16),
        ],
        compiler_params=pltpu.CompilerParams(vmem_limit_bytes=32 * 2**20),
        name="query_grads",
    )(tile_counts, gate, key_values, key_turned, received)


def image_grad_kernel(
    tiles_ref, gate_ref, key_value_ref, first_ref, second_ref, after_first, after_second,
    grad_key_ref, grad_value_ref,
    place_list, slot_list, key_sum, value_sum, query_cols, grad_cols, score_grads, weights,
):
    del after_first, after_second
    found = find_slots(first_ref, place_list, slot_list)
    key_sum[...] = jnp.zeros(key_sum.shape, jnp.float32)
    value_sum[...] = jnp.zeros(value_sum.shape, jnp.float32)

    def work(live):
        @pl.loop(0, (found + (GROUP - 1)) // GROUP)
        def _(block):
            for half, received in enumerate((first_ref, second_ref)):
                start = half * GROUP * DEPTH
                gather_block(block, found, place_list, received, query_cols, grad_cols, start)
                expos, grads, factors, delta = softmax_terms(
                    key_value_ref, live,
                    query_cols[start:start + SUB], grad_cols[start:start + SUB],
                    gate_ref[half:half + 1],
                )
                for number, (expo, grad, factor) in enumerate(zip(expos, grads, factors)):
                    rows = slice(number * CHUNK, (number + 1) * CHUNK)
                    weighted = expo * factor
                    score_grad = weighted * (grad - delta)
                    weights[rows, start:start + SUB] = (
                        weighted.reshape(CHUNK, SUB).astype(jnp.bfloat16)
                    )
                    score_grads[rows, start:start + SUB] = (
                        score_grad.reshape(CHUNK, SUB).astype(jnp.bfloat16)
                    )
            key_sum[:live] += nn_dot(score_grads[:live], query_cols[...])
            value_sum[:live] += nn_dot(weights[:live], grad_cols[...])

    most = key_value_ref.shape[0] // 2 // TILE
    for count in range(1, most + 1):
        @pl.when(tiles_ref[0] == count)
        def _(count=count):
            work(count * TILE)

    grad_key_ref[...] = (key_sum[...] * SCALE).astype(jnp.bfloat16)
    grad_value_ref[...] = value_sum[...].astype(jnp.bfloat16)


def image_grads(tile_counts, gate, key_values, first, second, after):
    slots = first.shape[0] // 2
    keys = key_values.shape[0] // 2
    cols = HALVES * GROUP * DEPTH
    smem = pl.BlockSpec(memory_space=pltpu.SMEM)
    vmem = pl.BlockSpec(memory_space=pltpu.VMEM)
    return pl.pallas_call(
        image_grad_kernel,
        out_shape=(
            jax.ShapeDtypeStruct((keys, HEAD), jnp.bfloat16),
            jax.ShapeDtypeStruct((keys, HEAD), jnp.bfloat16),
        ),
        in_specs=[smem, vmem, vmem, vmem, vmem] + [pl.BlockSpec(memory_space=pl.ANY)] * HALVES,
        out_specs=(vmem, vmem),
        scratch_shapes=[
            pltpu.SMEM((slots + GROUP,), jnp.int32),
            pltpu.SMEM((slots + GROUP,), jnp.int32),
            pltpu.VMEM((keys, HEAD), jnp.float32),
            pltpu.VMEM((keys, HEAD), jnp.float32),
            pltpu.VMEM((cols, HEAD), jnp.bfloat16),
            pltpu.VMEM((cols, HEAD), jnp.bfloat16),
            pltpu.VMEM((keys, cols), jnp.bfloat16),
            pltpu.VMEM((keys, cols), jnp.bfloat16),
        ],
        compiler_params=pltpu.CompilerParams(vmem_limit_bytes=32 * 2**20),
        cost_estimate=pl.CostEstimate(
            flops=8 * first.shape[0] * 16 * keys * HEAD,
            bytes_accessed=4 * 2**20,
            transcendentals=first.shape[0] * 16 * keys,
        ),
        name="image_grads",
    )(tile_counts, gate, key_values, first, second, *after)


def on_device(
    queries, grad_out, image_keys, image_values, gate_logits, tile_counts, owners, text_only
):
    rows, tokens, width = queries.shape
    heads = width // HEAD
    peers = lax.axis_size("dp")

    def slabs(array):
        split = array.reshape(rows, tokens, heads, HEAD).transpose(0, 2, 1, 3)
        return split.reshape(rows, heads * tokens, HEAD)

    *sends, slot_of = pack(owners[:, 0], text_only, slabs(queries), slabs(grad_out), peers)

    def exchange(array):
        return lax.all_to_all(array, "dp", split_axis=0, concat_axis=0, tiled=True)

    received = [exchange(send).reshape(peers * 2 * CAP, DEPTH, HEAD) for send in sends]
    key_values = jnp.concatenate([image_keys[0], image_values[0]])
    key_turned = image_keys[0].T
    gate = jnp.repeat(jnp.tanh(gate_logits), tokens).reshape(HALVES, DEPTH)
    gate = jnp.tile(gate, (1, SUB // DEPTH))
    grad_slots = [
        query_grads(tile_counts, gate[half:half + 1], key_values, key_turned, received[half])
        for half in range(HALVES)
    ]
    returned = [
        exchange(grads.reshape(peers, CAP, DEPTH, HEAD)).reshape(peers * CAP, DEPTH, HEAD)
        for grads in grad_slots
    ]
    grad_key, grad_value = image_grads(
        tile_counts, gate, key_values, received[0], received[1], grad_slots
    )
    grad_rows = unpack(slot_of, returned[0], returned[1])
    grad_rows = grad_rows.reshape(rows, heads, tokens, HEAD).transpose(0, 2, 1, 3)
    return grad_rows.reshape(rows, tokens, width), grad_key[None], grad_value[None]


def solution(mesh):
    placed = (
        P("dp", None, "tensor"),
        P("dp", None, "tensor"),
        P("dp", None, "tensor"),
        P("dp", None, "tensor"),
        P("tensor"),
        P("dp"),
        P("dp", None),
        P("dp"),
    )
    return jax.shard_map(
        on_device,
        mesh=mesh,
        in_specs=placed,
        out_specs=(P("dp", None, "tensor"), P("dp", None, "tensor"), P("dp", None, "tensor")),
        check_vma=False,
    )
```

time: 180 us -> 169 us (0.939)
  blocking collectives: 0 us -> 57.9 us
  waiting for transfers between devices: 104 us -> 56.8 us
  starting transfers between devices: 40.1 us -> 20.6 us
  Pallas kernels: 29.8 us -> 21.4 us
  local copies, waits for them, and re-layouts: 3.31 us -> 9.35 us
    all_to_all x0 -> x1, blocking collectives: none -> 57.9 us  [exchange(): return lax.all_to_all(array, 'dp', split_axis=0, concat_axis=0, tiled=True)]
    all_to_all x2 -> x3, waiting for transfers between devices: 104 us -> 56.8 us  [exchange(): return lax.all_to_all(array, 'dp', split_axis=0, concat_axis=0, tiled=True)]
    all_to_all x2 -> x3, starting transfers between devices: 40.1 us -> 20.6 us  [exchange(): return lax.all_to_all(array, 'dp', split_axis=0, concat_axis=0, tiled=True)]
    pallas_call x1 -> x2, Pallas kernels: 13 us -> 8.12 us  [query_grads(): pl.pallas_call(query_grad_kernel, out_shape=jax.ShapeDtypeStruct((slots,...]
    unnamed x18 -> x22, local copies, waits for them, and re-layouts: 1.68 us -> 6.32 us
    pallas_call x1, Pallas kernels: 10.1 us -> 6.5 us  [image_grads(): pl.pallas_call(image_grad_kernel, out_shape=(jax.ShapeDtypeStruct((keys,...]
  transfers between devices with their start and end apart: 2 -> 3, of which waited for: 2 -> 3; matrix products, arithmetic and copies ran while one was open for 1% -> 2% of each run, Pallas kernels for 6% -> 9%
where the time goes in v3:
time: 169 us; the launch traced here: 168 us
  blocking collectives  57.9 us (34%)
  waiting for transfers between devices  56.8 us (34%)
  Pallas kernels  21.4 us (13%)
  starting transfers between devices  20.6 us (12%)
  local copies, waits for them, and re-layouts  9.35 us (6%)
    all_to_all x1, blocking collectives, exchange(): return lax.all_to_all(array, 'dp', split_axis=0, concat_axis=0, tiled=True)  57.9 us
    all_to_all x3, waiting for transfers between devices, exchange(): return lax.all_to_all(array, 'dp', split_axis=0, concat_axis=0, tiled=True)  56.8 us
    all_to_all x3, starting transfers between devices, exchange(): return lax.all_to_all(array, 'dp', split_axis=0, concat_axis=0, tiled=True)  20.6 us
    pallas_call x2, Pallas kernels, query_grads(): pl.pallas_call(query_grad_kernel, out_shape=jax.ShapeDtypeStruct((slots,...  8.12 us
    pallas_call x1, Pallas kernels, image_grads(): pl.pallas_call(image_grad_kernel, out_shape=(jax.ShapeDtypeStruct((keys,...  6.5 us
    unnamed x22, local copies, waits for them, and re-layouts  6.32 us
    pallas_call x1, Pallas kernels, pack(): pl.pallas_call(pack_kernel, out_shape=(jax.ShapeDtypeStruct((peers, 2 * C...  4.1 us
  transfers between devices with their start and end apart: 3, of which 3 were waited for; matrix products, arithmetic and copies ran while one was open for 2% of the time, Pallas kernels for 9%

profile of v3, /device:TPU:6, one launch (start us, length us, event | category | flops | bytes accessed | tf_op | source)
XLA Modules:
  0.0 168.4 jit_solution(980839110449215961)
XLA Ops:
  0.6 4.1 %pack_rows.1 = (bf16[64,6,16,128]{3,2,1,0:T(8,128)(2,1)}, bf16[64,6,16,128]{3,2,1,0:T(8,128)(2,1)}, s32[128]{0:T(128)}) custom-call(s32[128]{0:T(128)} %bitcast.40, s32[128]{0:T(128)} %text_hbm.1, bf16[128,32,128]{2,1,0:T(8,128)(2,1)} %bitcast.35, bf16[128,32,128]{2,1,0:T(8,128)(2,1)} %bitcast.36), custom_call_target="tpu_custom_call" | custom-call | tf_op jit(solution)/shard_map/pack_rows/pallas_call | solution.py:85
  4.7 57.9 %all_to_all.20 = bf16[64,6,16,128]{3,2,1,0:T(8,128)(2,1)S(1)} all-to-all(bf16[64,6,16,128]{3,2,1,0:T(8,128)(2,1)} %get-tuple-element.9), channel_id=1, replica_groups=mesh['dp'=64,'tensor'=8] {'dp'}, dimensions={0} | all-to-all | bytes 3145728 | tf_op jit(solution)/shard_map/all_to_all | solution.py:364
  62.6 7.7 %all-to-all-start.2 = ((bf16[64,6,16,128]{3,2,1,0:T(8,128)(2,1)}), bf16[64,6,16,128]{3,2,1,0:T(8,128)(2,1)S(1)}, u32[]{:S(2)}, u32[]{:S(2)}) async-start(bf16[64,6,16,128]{3,2,1,0:T(8,128)(2,1)} %get-tuple-element.10), calls=%async_computation.2 | async-start | bytes 3145728 | tf_op jit(solution)/shard_map/all_to_all | solution.py:364
  70.4 0.1 fusion
  70.5 0.4 copy-done.8
  71.0 0.1 broadcast_in_dim.22
  71.1 0.1 tile.17.gate_ref
  71.8 0.8 copy.13.turned_ref
  72.6 1.0 pad_maximum_fusion.key_value_ref
  73.7 0.9 copy-done.4
  74.6 4.1 %query_grads.2.after_first = bf16[192,16,128]{2,1,0:T(8,128)(2,1)S(1)} custom-call(s32[1]{0:T(128)S(6)} %copy.16.tiles_ref, f32[1,256]{1,0:T(1,128)S(1)} %tile.17.gate_ref, bf16[1536,128]{1,0:T(8,128)(2,1)S(1)} %pad_maximum_fusion.key_value_ref, bf16[128,768]{1,0:T(8,128)(2,1)S(1)} %copy-done.4, bf16[384,16,128]{2,1,0:T(8,128)(2,1)S(1)} %bitcast.28), custom_call_target="tpu_custom_call" | custom-call | tf_op jit(solution)/shard_map/query_grads/pallas_call | solution.py:255
  78.7 0.9 copy-done
  79.6 30.3 %all-to-all-done.2 = bf16[64,6,16,128]{3,2,1,0:T(8,128)(2,1)S(1)} async-done(((bf16[64,6,16,128]{3,2,1,0:T(8,128)(2,1)}), bf16[64,6,16,128]{3,2,1,0:T(8,128)(2,1)S(1)}, u32[]{:S(2)}, u32[]{:S(2)}) %all-to-all-start.2) | async-done | bytes 1572896 | tf_op jit(solution)/shard_map/all_to_all | solution.py:364
  109.8 6.8 %all-to-all-start.1 = ((bf16[64,3,16,128]{3,2,1,0:T(8,128)(2,1)}), bf16[64,3,16,128]{3,2,1,0:T(8,128)(2,1)}, u32[]{:S(2)}, u32[]{:S(2)}) async-start(bf16[64,3,16,128]{3,2,1,0:T(8,128)(2,1)} %bitcast.32), calls=%async_computation.1 | async-start | bytes 1572864 | tf_op jit(solution)/shard_map/all_to_all | solution.py:364
  116.7 0.1 broadcast_in_dim.23
  116.8 0.1 broadcast_in_dim.24
  116.9 0.1 tile.19.gate_ref
  116.9 0.9 copy-done.5
  117.9 4.1 %query_grads.3.after_second = bf16[192,16,128]{2,1,0:T(8,128)(2,1)S(1)} custom-call(s32[1]{0:T(128)S(6)} %copy.16.tiles_ref, f32[1,256]{1,0:T(1,128)S(1)} %tile.19.gate_ref, bf16[1536,128]{1,0:T(8,128)(2,1)S(1)} %pad_maximum_fusion.key_value_ref, bf16[128,768]{1,0:T(8,128)(2,1)S(1)} %copy-done.5, bf16[384,16,128]{2,1,0:T(8,128)(2,1)S(1)} %bitcast.30), custom_call_target="tpu_custom_call" | custom-call | tf_op jit(solution)/shard_map/query_grads/pallas_call | solution.py:255
  122.0 0.9 copy-done.2
  122.8 15.8 %all-to-all-done.1 = bf16[64,3,16,128]{3,2,1,0:T(8,128)(2,1)} async-done(((bf16[64,3,16,128]{3,2,1,0:T(8,128)(2,1)}), bf16[64,3,16,128]{3,2,1,0:T(8,128)(2,1)}, u32[]{:S(2)}, u32[]{:S(2)}) %all-to-all-start.1) | async-done | bytes 786464 | tf_op jit(solution)/shard_map/all_to_all | solution.py:364
  138.7 6.0 %all-to-all-start.3 = ((bf16[64,3,16,128]{3,2,1,0:T(8,128)(2,1)}), bf16[64,3,16,128]{3,2,1,0:T(8,128)(2,1)}, u32[]{:S(2)}, u32[]{:S(2)}) async-start(bf16[64,3,16,128]{3,2,1,0:T(8,128)(2,1)} %bitcast.33), calls=%async_computation.3 | async-start | bytes 1572864 | tf_op jit(solution)/shard_map/all_to_all | solution.py:364
  144.7 0.1 broadcast_in_dim.25
  144.7 0.1 broadcast_in_dim.26
  144.8 0.1 broadcast_in_dim.27
  144.9 0.6 tile.20
  145.5 0.8 tile.21.gate_ref
  146.3 1.1 copy-done.1
  147.5 1.1 copy-done.3
  148.6 6.5 %image_grads.1 = (bf16[768,128]{1,0:T(8,128)(2,1)}, bf16[768,128]{1,0:T(8,128)(2,1)}) custom-call(s32[1]{0:T(128)S(6)} %copy.16.tiles_ref, f32[2,256]{1,0:T(2,128)S(1)} %tile.21.gate_ref, bf16[1536,128]{1,0:T(8,128)(2,1)S(1)} %pad_maximum_fusion.key_value_ref, bf16[384,16,128]{2,1,0:T(8,128)(2,1)S(1)} %bitcast.29, bf16[384,16,128]{2,1,0:T(8,128)(2,1)S(1)} %bitcast.31, ...), custom_call_target="tpu_custom_call" | custom-call | flops 4831838208 | bytes 4194304 | tf_op jit(solution)/shard_map/image_grads/pallas_call | solution.py:322
  155.1 10.7 %all-to-all-done.3 = bf16[64,3,16,128]{3,2,1,0:T(8,128)(2,1)} async-done(((bf16[64,3,16,128]{3,2,1,0:T(8,128)(2,1)}), bf16[64,3,16,128]{3,2,1,0:T(8,128)(2,1)}, u32[]{:S(2)}, u32[]{:S(2)}) %all-to-all-start.3) | async-done | bytes 786464 | tf_op jit(solution)/shard_map/all_to_all | solution.py:364
  165.7 2.6 %unpack_rows.1 = bf16[128,32,128]{2,1,0:T(8,128)(2,1)} custom-call(s32[128]{0:T(128)S(1)} %copy-done.6, bf16[192,16,128]{2,1,0:T(8,128)(2,1)} %bitcast.12.first_ref, bf16[192,16,128]{2,1,0:T(8,128)(2,1)} %bitcast.15.second_ref), custom_call_target="tpu_custom_call" | custom-call | tf_op jit(solution)/shard_map/unpack_rows/pallas_call | solution.py:139
  (19 shorter events, 0.1 us)
Async XLA Ops:
  62.6 7.7 %copy-start.10 = (f32[8]{0:T(128)S(1)}, f32[8]{0:T(128)}, u32[]{:S(2)}) copy-start(f32[8]{0:T(128)} %param.12) | copy-start | bytes 100
  62.6 9.2 %copy-start.7 = (bf16[1,768,128]{2,1,0:T(8,128)(2,1)S(1)}, bf16[1,768,128]{2,1,0:T(8,128)(2,1)}, u32[]{:S(2)}) copy-start(bf16[1,768,128]{2,1,0:T(8,128)(2,1)} %param.10) | copy-start | bytes 589828
  62.6 47.2 %all-to-all-start.2 = ((bf16[64,6,16,128]{3,2,1,0:T(8,128)(2,1)}), bf16[64,6,16,128]{3,2,1,0:T(8,128)(2,1)S(1)}, u32[]{:S(2)}, u32[]{:S(2)}) async-start(bf16[64,6,16,128]{3,2,1,0:T(8,128)(2,1)} %get-tuple-element.10), calls=%async_computation.2 | async-start | bytes 3145728 | tf_op jit(solution)/shard_map/all_to_all | solution.py:364
  70.4 0.5 copy-start.8
  73.7 0.9 copy-start.4
  78.7 0.9 copy-start
  109.8 28.8 %all-to-all-start.1 = ((bf16[64,3,16,128]{3,2,1,0:T(8,128)(2,1)}), bf16[64,3,16,128]{3,2,1,0:T(8,128)(2,1)}, u32[]{:S(2)}, u32[]{:S(2)}) async-start(bf16[64,3,16,128]{3,2,1,0:T(8,128)(2,1)} %bitcast.32), calls=%async_computation.1 | async-start | bytes 1572864 | tf_op jit(solution)/shard_map/all_to_all | solution.py:364
  116.9 0.9 copy-start.5
  117.9 26.8 %copy-start.9 = (f32[8]{0:T(128)S(1)}, f32[8]{0:T(128)}, u32[]{:S(2)}) copy-start(f32[8]{0:T(128)} %copy-done.8) | copy-start | bytes 100
  121.9 0.9 copy-start.2
  138.7 27.1 %all-to-all-start.3 = ((bf16[64,3,16,128]{3,2,1,0:T(8,128)(2,1)}), bf16[64,3,16,128]{3,2,1,0:T(8,128)(2,1)}, u32[]{:S(2)}, u32[]{:S(2)}) async-start(bf16[64,3,16,128]{3,2,1,0:T(8,128)(2,1)} %bitcast.33), calls=%async_computation.3 | async-start | bytes 1572864 | tf_op jit(solution)/shard_map/all_to_all | solution.py:364
  146.3 1.1 copy-start.1
  147.5 1.1 copy-start.3
  148.6 17.2 %copy-start.6 = (s32[128]{0:T(128)S(1)}, s32[128]{0:T(128)}, u32[]{:S(2)}) copy-start(s32[128]{0:T(128)} %get-tuple-element.8.slot_ref) | copy-start | bytes 1540

commit v4 on v3

--- a/solution.py
+++ b/solution.py
@@ -347,6 +347,36 @@
     )(tile_counts, gate, key_values, first, second, *after)
 
 
+def prepare_kernel(key_ref, value_ref, send_in, send_out, key_value_ref, turned_ref):
+    del send_in, send_out
+    keys = key_ref.shape[0]
+    key_value_ref[:keys] = key_ref[...]
+    key_value_ref[keys:] = value_ref[...]
+    turned_ref[...] = key_ref[...].T
+
+
+def prepare(key_rows, value_rows, send):
+    keys = key_rows.shape[0]
+    vmem = pl.BlockSpec(memory_space=pltpu.VMEM)
+    hbm = pl.BlockSpec(memory_space=pltpu.HBM)
+    return pl.pallas_call(
+        prepare_kernel,
+        out_shape=(
+            jax.ShapeDtypeStruct(send.shape, send.dtype),
+            jax.ShapeDtypeStruct((2 * keys, HEAD), jnp.bfloat16),
+            jax.ShapeDtypeStruct((HEAD, keys), jnp.bfloat16),
+        ),
+        in_specs=[vmem, vmem, hbm],
+        out_specs=(hbm, vmem, vmem),
+        input_output_aliases={2: 0},
+        compiler_params=pltpu.CompilerParams(vmem_limit_bytes=60 * 2**20),
+        cost_estimate=pl.CostEstimate(
+            flops=0, bytes_accessed=6 * 2 * keys * HEAD, transcendentals=0
+        ),
+        name="prepare_keys",
+    )(key_rows, value_rows, send)
+
+
 def on_device(
     queries, grad_out, image_keys, image_values, gate_logits, tile_counts, owners, text_only
 ):
@@ -363,9 +393,8 @@
     def exchange(array):
         return lax.all_to_all(array, "dp", split_axis=0, concat_axis=0, tiled=True)
 
+    sends[1], key_values, key_turned = prepare(image_keys[0], image_values[0], sends[1])
     received = [exchange(send).reshape(peers * 2 * CAP, DEPTH, HEAD) for send in sends]
-    key_values = jnp.concatenate([image_keys[0], image_values[0]])
-    key_turned = image_keys[0].T
     gate = jnp.repeat(jnp.tanh(gate_logits), tokens).reshape(HALVES, DEPTH)
     gate = jnp.tile(gate, (1, SUB // DEPTH))
     grad_slots = [

time: 169 us -> 171 us (1.012)
  Pallas kernels: 21.4 us -> 23.3 us
    pallas_call x0 -> x1, Pallas kernels: none -> 1.89 us  [prepare(): pl.pallas_call(prepare_kernel, out_shape=(jax.ShapeDtypeStruct(send.shape...]
    all_to_all x3, waiting for transfers between devices: 56.8 us -> 58.5 us  [exchange(): return lax.all_to_all(array, 'dp', split_axis=0, concat_axis=0, tiled=True)]
    unnamed x22 -> x24, local copies, waits for them, and re-layouts: 6.32 us -> 5.93 us
where the time goes in v4:
time: 171 us; the launch traced here: 170 us
  waiting for transfers between devices  58.5 us (34%)
  blocking collectives  57.9 us (34%)
  Pallas kernels  23.3 us (14%)
  starting transfers between devices  20.6 us (12%)
  local copies, waits for them, and re-layouts  8.59 us (5%)
    all_to_all x3, waiting for transfers between devices, exchange(): return lax.all_to_all(array, 'dp', split_axis=0, concat_axis=0, tiled=True)  58.5 us
    all_to_all x1, blocking collectives, exchange(): return lax.all_to_all(array, 'dp', split_axis=0, concat_axis=0, tiled=True)  57.9 us
    all_to_all x3, starting transfers between devices, exchange(): return lax.all_to_all(array, 'dp', split_axis=0, concat_axis=0, tiled=True)  20.6 us
    pallas_call x2, Pallas kernels, query_grads(): pl.pallas_call(query_grad_kernel, out_shape=jax.ShapeDtypeStruct((slots,...  8.13 us
    pallas_call x1, Pallas kernels, image_grads(): pl.pallas_call(image_grad_kernel, out_shape=(jax.ShapeDtypeStruct((keys,...  6.52 us
    unnamed x24, local copies, waits for them, and re-layouts  5.93 us
    pallas_call x1, Pallas kernels, pack(): pl.pallas_call(pack_kernel, out_shape=(jax.ShapeDtypeStruct((peers, 2 * C...  4.13 us
  transfers between devices with their start and end apart: 3, of which 3 were waited for; matrix products, arithmetic and copies ran while one was open for 2% of the time, Pallas kernels for 9%

profile of v4, /device:TPU:6, one launch (start us, length us, event | category | flops | bytes accessed | tf_op | source)
XLA Modules:
  0.0 170.3 jit_solution(9089053438638049039)
XLA Ops:
  0.6 4.1 %pack_rows.1 = (bf16[64,6,16,128]{3,2,1,0:T(8,128)(2,1)}, bf16[64,6,16,128]{3,2,1,0:T(8,128)(2,1)}, s32[128]{0:T(128)}) custom-call(s32[128]{0:T(128)} %bitcast.37, s32[128]{0:T(128)} %text_hbm.1, bf16[128,32,128]{2,1,0:T(8,128)(2,1)} %bitcast.33, bf16[128,32,128]{2,1,0:T(8,128)(2,1)} %bitcast.34), custom_call_target="tpu_custom_call" | custom-call | tf_op jit(solution)/shard_map/pack_rows/pallas_call | solution.py:85
  4.8 1.9 %prepare_keys.1 = (bf16[64,6,16,128]{3,2,1,0:T(8,128)(2,1)}, bf16[1536,128]{1,0:T(8,128)(2,1)}, bf16[128,768]{1,0:T(8,128)(2,1)}) custom-call(bf16[768,128]{1,0:T(8,128)(2,1)} %bitcast.35, bf16[768,128]{1,0:T(8,128)(2,1)} %bitcast.36, bf16[64,6,16,128]{3,2,1,0:T(8,128)(2,1)} %get-tuple-element.12.send_in), custom_call_target="tpu_custom_call", output_to_operand_aliasing={{0}: (2, {})} | custom-call | bytes 1179648 | tf_op jit(solution)/shard_map/prepare_keys/pallas_call | solution.py:362
  6.7 57.9 %all_to_all.20 = bf16[64,6,16,128]{3,2,1,0:T(8,128)(2,1)S(1)} all-to-all(bf16[64,6,16,128]{3,2,1,0:T(8,128)(2,1)} %get-tuple-element.16), channel_id=1, replica_groups=mesh['dp'=64,'tensor'=8] {'dp'}, dimensions={0} | all-to-all | bytes 3145728 | tf_op jit(solution)/shard_map/all_to_all | solution.py:394
  64.5 7.7 %all-to-all-start = ((bf16[64,6,16,128]{3,2,1,0:T(8,128)(2,1)}), bf16[64,6,16,128]{3,2,1,0:T(8,128)(2,1)S(1)}, u32[]{:S(2)}, u32[]{:S(2)}) async-start(bf16[64,6,16,128]{3,2,1,0:T(8,128)(2,1)} %get-tuple-element.15), calls=%async_computation | async-start | bytes 3145728 | tf_op jit(solution)/shard_map/all_to_all | solution.py:394
  72.3 0.5 fusion
  72.8 0.1 copy-done.8
  72.9 0.1 broadcast_in_dim.23
  72.9 0.1 broadcast_in_dim.24
  73.0 0.1 tile.19.gate_ref
  73.8 0.9 copy-done.5
  74.7 4.1 %query_grads.3.after_second = bf16[192,16,128]{2,1,0:T(8,128)(2,1)S(1)} custom-call(s32[1]{0:T(128)S(6)} %copy.16.tiles_ref, f32[1,256]{1,0:T(1,128)S(1)} %tile.19.gate_ref, bf16[1536,128]{1,0:T(8,128)(2,1)S(1)} %copy-done.4, bf16[128,768]{1,0:T(8,128)(2,1)S(1)} %copy-done.5, bf16[384,16,128]{2,1,0:T(8,128)(2,1)S(1)} %bitcast.26), custom_call_target="tpu_custom_call" | custom-call | tf_op jit(solution)/shard_map/query_grads/pallas_call | solution.py:255
  78.8 0.9 copy-done
  79.7 32.1 %all-to-all-done = bf16[64,6,16,128]{3,2,1,0:T(8,128)(2,1)S(1)} async-done(((bf16[64,6,16,128]{3,2,1,0:T(8,128)(2,1)}), bf16[64,6,16,128]{3,2,1,0:T(8,128)(2,1)S(1)}, u32[]{:S(2)}, u32[]{:S(2)}) %all-to-all-start) | async-done | bytes 1572896 | tf_op jit(solution)/shard_map/all_to_all | solution.py:394
  111.7 6.8 %all-to-all-start.3 = ((bf16[64,3,16,128]{3,2,1,0:T(8,128)(2,1)}), bf16[64,3,16,128]{3,2,1,0:T(8,128)(2,1)}, u32[]{:S(2)}, u32[]{:S(2)}) async-start(bf16[64,3,16,128]{3,2,1,0:T(8,128)(2,1)} %bitcast.30), calls=%async_computation.3 | async-start | bytes 1572864 | tf_op jit(solution)/shard_map/all_to_all | solution.py:394
  118.6 0.1 broadcast_in_dim.21
  118.7 0.1 broadcast_in_dim.22
  118.8 0.1 tile.17.gate_ref
  118.9 0.9 copy-done.6
  119.8 4.1 %query_grads.2.after_first = bf16[192,16,128]{2,1,0:T(8,128)(2,1)S(1)} custom-call(s32[1]{0:T(128)S(6)} %copy.16.tiles_ref, f32[1,256]{1,0:T(1,128)S(1)} %tile.17.gate_ref, bf16[1536,128]{1,0:T(8,128)(2,1)S(1)} %copy-done.4, bf16[128,768]{1,0:T(8,128)(2,1)S(1)} %copy-done.6, bf16[384,16,128]{2,1,0:T(8,128)(2,1)S(1)} %bitcast.28), custom_call_target="tpu_custom_call" | custom-call | tf_op jit(solution)/shard_map/query_grads/pallas_call | solution.py:255
  123.9 0.9 copy-done.2
  124.7 15.8 %all-to-all-done.3 = bf16[64,3,16,128]{3,2,1,0:T(8,128)(2,1)} async-done(((bf16[64,3,16,128]{3,2,1,0:T(8,128)(2,1)}), bf16[64,3,16,128]{3,2,1,0:T(8,128)(2,1)}, u32[]{:S(2)}, u32[]{:S(2)}) %all-to-all-start.3) | async-done | bytes 786464 | tf_op jit(solution)/shard_map/all_to_all | solution.py:394
  140.6 6.0 %all-to-all-start.1 = ((bf16[64,3,16,128]{3,2,1,0:T(8,128)(2,1)}), bf16[64,3,16,128]{3,2,1,0:T(8,128)(2,1)}, u32[]{:S(2)}, u32[]{:S(2)}) async-start(bf16[64,3,16,128]{3,2,1,0:T(8,128)(2,1)} %bitcast.31), calls=%async_computation.1 | async-start | bytes 1572864 | tf_op jit(solution)/shard_map/all_to_all | solution.py:394
  146.6 0.1 broadcast_in_dim.25
  146.7 0.1 broadcast_in_dim.26
  146.7 0.1 broadcast_in_dim.27
  146.8 0.6 tile.20
  147.4 0.8 tile.21.gate_ref
  148.2 1.1 copy-done.1
  149.4 1.1 copy-done.3
  150.5 6.5 %image_grads.1 = (bf16[768,128]{1,0:T(8,128)(2,1)}, bf16[768,128]{1,0:T(8,128)(2,1)}) custom-call(s32[1]{0:T(128)S(6)} %copy.16.tiles_ref, f32[2,256]{1,0:T(2,128)S(1)} %tile.21.gate_ref, bf16[1536,128]{1,0:T(8,128)(2,1)S(1)} %copy-done.4, bf16[384,16,128]{2,1,0:T(8,128)(2,1)S(1)} %bitcast.29, bf16[384,16,128]{2,1,0:T(8,128)(2,1)S(1)} %bitcast.27, ...), custom_call_target="tpu_custom_call" | custom-call | flops 4831838208 | bytes 4194304 | tf_op jit(solution)/shard_map/image_grads/pallas_call | solution.py:322
  157.0 10.6 %all-to-all-done.1 = bf16[64,3,16,128]{3,2,1,0:T(8,128)(2,1)} async-done(((bf16[64,3,16,128]{3,2,1,0:T(8,128)(2,1)}), bf16[64,3,16,128]{3,2,1,0:T(8,128)(2,1)}, u32[]{:S(2)}, u32[]{:S(2)}) %all-to-all-start.1) | async-done | bytes 786464 | tf_op jit(solution)/shard_map/all_to_all | solution.py:394
  167.7 2.6 %unpack_rows.1 = bf16[128,32,128]{2,1,0:T(8,128)(2,1)} custom-call(s32[128]{0:T(128)S(1)} %copy-done.7, bf16[192,16,128]{2,1,0:T(8,128)(2,1)} %bitcast.11.first_ref, bf16[192,16,128]{2,1,0:T(8,128)(2,1)} %bitcast.14.second_ref), custom_call_target="tpu_custom_call" | custom-call | tf_op jit(solution)/shard_map/unpack_rows/pallas_call | solution.py:139
  (20 shorter events, 0.1 us)
Async XLA Ops:
  64.5 7.7 %copy-start.11 = (f32[8]{0:T(128)S(1)}, f32[8]{0:T(128)}, u32[]{:S(2)}) copy-start(f32[8]{0:T(128)} %param.12) | copy-start | bytes 100
  64.5 9.2 %copy-start.4 = (bf16[1536,128]{1,0:T(8,128)(2,1)S(1)}, bf16[1536,128]{1,0:T(8,128)(2,1)}, u32[]{:S(2)}) copy-start(bf16[1536,128]{1,0:T(8,128)(2,1)} %get-tuple-element.13.key_value_ref) | copy-start | bytes 1179652
  64.5 47.2 %all-to-all-start = ((bf16[64,6,16,128]{3,2,1,0:T(8,128)(2,1)}), bf16[64,6,16,128]{3,2,1,0:T(8,128)(2,1)S(1)}, u32[]{:S(2)}, u32[]{:S(2)}) async-start(bf16[64,6,16,128]{3,2,1,0:T(8,128)(2,1)} %get-tuple-element.15), calls=%async_computation | async-start | bytes 3145728 | tf_op jit(solution)/shard_map/all_to_all | solution.py:394
  72.3 0.6 copy-start.8
  73.8 0.9 copy-start.5
  74.7 43.9 %copy-start.10 = (f32[4]{0:T(128)S(1)}, f32[4]{0:T(128)}, u32[]{:S(2)}) copy-start(f32[4]{0:T(128)} %get-tuple-element.20) | copy-start | bytes 52
  78.8 0.9 copy-start
  111.7 28.8 %all-to-all-start.3 = ((bf16[64,3,16,128]{3,2,1,0:T(8,128)(2,1)}), bf16[64,3,16,128]{3,2,1,0:T(8,128)(2,1)}, u32[]{:S(2)}, u32[]{:S(2)}) async-start(bf16[64,3,16,128]{3,2,1,0:T(8,128)(2,1)} %bitcast.30), calls=%async_computation.3 | async-start | bytes 1572864 | tf_op jit(solution)/shard_map/all_to_all | solution.py:394
  118.9 0.9 copy-start.6
  119.8 26.8 %copy-start.9 = (f32[8]{0:T(128)S(1)}, f32[8]{0:T(128)}, u32[]{:S(2)}) copy-start(f32[8]{0:T(128)} %copy-done.8) | copy-start | bytes 100
  123.9 0.9 copy-start.2
  140.6 27.1 %all-to-all-start.1 = ((bf16[64,3,16,128]{3,2,1,0:T(8,128)(2,1)}), bf16[64,3,16,128]{3,2,1,0:T(8,128)(2,1)}, u32[]{:S(2)}, u32[]{:S(2)}) async-start(bf16[64,3,16,128]{3,2,1,0:T(8,128)(2,1)} %bitcast.31), calls=%async_computation.1 | async-start | bytes 1572864 | tf_op jit(solution)/shard_map/all_to_all | solution.py:394
  148.2 1.1 copy-start.1
  149.4 1.1 copy-start.3
  150.5 17.2 %copy-start.7 = (s32[128]{0:T(128)S(1)}, s32[128]{0:T(128)}, u32[]{:S(2)}) copy-start(s32[128]{0:T(128)} %get-tuple-element.11.slot_ref) | copy-start | bytes 1540
